TPU v7x, 256 devices: a whole 4x4x8 slice. The times are simulated.
256 devices in a mesh: row: 16 (over y, z_lo, core), col: 16 (over x, z_hi).
Axes of the slice: x: 4, y: 4, z: 8 (z_hi: 4, z_lo: 2; z = z_hi * 2 + z_lo), core: 2. Of those that a mesh axis runs over, the one named last changes fastest.
Arguments:
- positions: float32 [4096, 147], P(('row', 'col')), may hold values from -0.55 to 9.45, as said below
- coefficients: float32 [4096, 147], P(('row', 'col')), may hold values from -6 to 6
- atom_pairs: int32 [2, 1176], replicated, may hold values from 0 to 48, as said below
- pair_scale: float32 [1176], replicated, may hold values from 0.5 to 2
Outputs:
- applied: float32 [4096, 147], P(('row', 'col'))
Inputs may be any that keep to these rules, and one draw needn't show every extreme that they name: `atom_pairs`: every unordered pair of two different atoms stands in exactly one column, the smaller atom in row 0. `positions`: every two atoms of a geometry lie 0.6 or more apart; all geometries are displacements of one molecule.
All inputs are finite; a program needn't handle non-finite values.
Results may differ from a plain program's by a relative error of at most 0.0003.
Values sent between devices are 32-bit elements; how exact they have to be, the bound alone decides.
No kernel may reach another device: no remote copies, remote signals or barrier semaphores. Data moves between devices by JAX's collectives and lax.ppermute only.
A program may use at most 64 MiB of HBM per device.

v0:
```python
import math

import jax
import jax.numpy as jnp
from jax import lax
from jax.sharding import PartitionSpec as P

highest = lax.Precision.HIGHEST
length_scale = 2.0
decay_rate = math.sqrt(5.0) / length_scale
outer_factor = decay_rate * decay_rate / 3.0
radial_factor = decay_rate * decay_rate


def from_everyone(value, axis):
    copies = jnp.broadcast_to(value, (lax.axis_size(axis), *value.shape))
    return lax.all_to_all(copies, axis, split_axis=0, concat_axis=0, tiled=True)


def joined_along(parts, dim):
    parts = jnp.moveaxis(parts, 0, dim)
    lengths = parts.shape
    return parts.reshape(*lengths[:dim], lengths[dim] * lengths[dim + 1], *lengths[dim + 2 :])


def gather_directly(value, axis, dim):
    parts = from_everyone(value, axis)
    return joined_along(parts, dim)


def sent_together(arrays, axis, dim, along):
    widths = [a.shape[along] for a in arrays]
    both = jnp.concatenate(arrays, axis=along)
    whole = gather_directly(both, axis, dim)
    return tuple(jnp.split(whole, [sum(widths[:k]) for k in range(1, len(widths))], axis=along))


def sent_together_2(arrays, axis, dim, along):
    ends, at = ([], 0)
    for a in arrays[:-1]:
        at += a.shape[along]
        ends.append(at)
    both = jnp.concatenate(arrays, axis=along)
    return tuple(jnp.split(lax.all_gather(both, axis, axis=dim, tiled=True), ends, axis=along))


def cut_along(value, dim, peers):
    before, after = (value.shape[:dim], value.shape[dim + 1 :])
    return jnp.moveaxis(value.reshape(*before, peers, -1, *after), dim, 0)


def sum_at_owner(value, axis, dim):
    parts = cut_along(value, dim, lax.axis_size(axis))
    arrived = lax.all_to_all(parts, axis, split_axis=0, concat_axis=0, tiled=True)
    return arrived.sum(axis=0)


def pair_table(atom_pairs, atoms):
    atom_ids = jnp.arange(atoms, dtype=jnp.int32)[:, None]
    first = (atom_ids == atom_pairs[0][None, :]).astype(jnp.float32)
    second = (atom_ids == atom_pairs[1][None, :]).astype(jnp.float32)
    return first - second


def geometry_terms(positions, coefficients, onehot, pair_scale):
    count = positions.shape[0]
    atoms = onehot.shape[0]
    spans = jnp.dot(positions.reshape(count * 3, atoms), onehot, precision=highest).reshape(
        count, 3, -1
    )
    moves = jnp.dot(coefficients.reshape(count * 3, atoms), onehot, precision=highest).reshape(
        count, 3, -1
    )
    inverse = 1.0 / jnp.sqrt(jnp.sum(spans * spans, axis=1))
    features = pair_scale[None, :] * inverse
    weights = features * inverse * inverse
    tangents = -weights * jnp.sum(spans * moves, axis=1)
    return (features, tangents, spans, weights)


def pull_back(grads, spans, weights, onehot):
    count = grads.shape[0]
    terms = -(weights * grads)[:, None, :] * spans
    return jnp.dot(terms.reshape(count * 3, -1), onehot.T, precision=highest).reshape(count, -1)


def kernel_terms(rows_x, cols_x):
    gram = jnp.dot(rows_x, cols_x.T, precision=highest)
    sq_dist = (
        jnp.sum(rows_x * rows_x, axis=1)[:, None]
        + jnp.sum(cols_x * cols_x, axis=1)[None, :]
        - 2.0 * gram
    )
    radius = jnp.sqrt(jnp.maximum(sq_dist, 0.0))
    envelope = outer_factor * jnp.exp(-decay_rate * radius)
    return (envelope, envelope * (1.0 + decay_rate * radius))


def both_ways(rows_x, rows_u, cols_x, cols_u, tile_weight):
    envelope, direct = kernel_terms(rows_x, cols_x)
    envelope = envelope * tile_weight
    direct = direct * tile_weight
    forward = envelope * (
        jnp.dot(rows_x, cols_u.T, precision=highest) - jnp.sum(cols_x * cols_u, axis=1)[None, :]
    )
    backward = envelope * (
        jnp.dot(rows_u, cols_x.T, precision=highest) - jnp.sum(rows_x * rows_u, axis=1)[:, None]
    )
    to_rows = jnp.dot(direct, cols_u, precision=highest) - radial_factor * (
        jnp.sum(forward, axis=1)[:, None] * rows_x - jnp.dot(forward, cols_x, precision=highest)
    )
    to_cols = jnp.dot(direct.T, rows_u, precision=highest) - radial_factor * (
        jnp.sum(backward, axis=0)[:, None] * cols_x - jnp.dot(backward.T, rows_x, precision=highest)
    )
    return (to_rows, to_cols)


def kept_blocks(col_count, col_index, kept_span):
    steps = jnp.arange(kept_span, dtype=jnp.int32)
    return (col_index - steps) % col_count


def select_rows(block, col_count, col_index, kept_span):
    pieces = block.reshape(col_count, -1, block.shape[1])
    kept = jnp.take(pieces, kept_blocks(col_count, col_index, kept_span), axis=0)
    return kept.reshape(-1, block.shape[1])


def restore_rows(block, col_count, col_index, kept_span):
    pieces = block.reshape(kept_span, -1, block.shape[1])
    chosen = kept_blocks(col_count, col_index, kept_span)
    placing = (jnp.arange(col_count, dtype=jnp.int32)[:, None] == chosen[None, :]).astype(
        pieces.dtype
    )
    padded = jnp.einsum("ck,kgf->cgf", placing, pieces, precision=highest)
    return padded.reshape(-1, block.shape[1])


def fold_weights(row_count, col_count, row_index, col_index, per_device):
    kept_half = col_count // 2
    offsets = jnp.arange(kept_half + 1, dtype=jnp.int32)[:, None]
    partner = jnp.arange(row_count, dtype=jnp.int32)[None, :]
    apart = (partner - row_index) % row_count
    first = jnp.where(
        apart == 0,
        0.5,
        jnp.where(
            (apart >= 1) & (apart < row_count // 2),
            1.0,
            jnp.where((apart == row_count // 2) & (row_index < partner), 1.0, 0.0),
        ),
    )
    middle = jnp.where(
        (row_index < partner) | (row_index == partner) & (col_index < kept_half), 1.0, 0.0
    )
    chosen = jnp.where(offsets == 0, first, jnp.where(offsets == kept_half, middle, 1.0)).astype(
        jnp.float32
    )
    spread = jnp.broadcast_to(
        chosen[:, None, :, None], (kept_half + 1, per_device, row_count, per_device)
    )
    return spread.reshape((kept_half + 1) * per_device, row_count * per_device)


def on_device(positions, coefficients, atom_pairs, pair_scale):
    row_count = lax.axis_size("row")
    col_count = lax.axis_size("col")
    row_index = lax.axis_index("row")
    col_index = lax.axis_index("col")
    per_device = positions.shape[0]
    atoms = positions.shape[1] // 3
    kept_span = col_count // 2 + 1
    onehot = pair_table(atom_pairs, atoms)
    tile_weight = fold_weights(row_count, col_count, row_index, col_index, per_device)
    rows_p, rows_c = sent_together((positions, coefficients), "col", 0, 1)
    cols_p, cols_c = sent_together_2((positions, coefficients), "row", 0, 1)
    rows_p = select_rows(rows_p, col_count, col_index, kept_span)
    rows_c = select_rows(rows_c, col_count, col_index, kept_span)
    rows_x, rows_u, rows_span, rows_weight = geometry_terms(rows_p, rows_c, onehot, pair_scale)
    cols_x, cols_u, cols_span, cols_weight = geometry_terms(cols_p, cols_c, onehot, pair_scale)
    to_rows, to_cols = both_ways(rows_x, rows_u, cols_x, cols_u, tile_weight)
    row_cart = restore_rows(
        pull_back(to_rows, rows_span, rows_weight, onehot), col_count, col_index, kept_span
    )
    col_cart = pull_back(to_cols, cols_span, cols_weight, onehot)
    own_rows = sum_at_owner(row_cart, "col", 0)
    own_cols = sum_at_owner(col_cart, "row", 0)
    return own_rows + own_cols


def solution(mesh):
    in_specs = (P(("row", "col"), None), P(("row", "col"), None), P(), P())
    out_specs = P(("row", "col"), None)
    return jax.shard_map(
        on_device, mesh=mesh, in_specs=in_specs, out_specs=out_specs, check_vma=False
    )
```

profile of v0, /device:TPU:1, one launch (start us, length us, event | category | flops | bytes accessed | tf_op | source)
XLA Modules:
  0.0 130.4 jit_solution(4894086283601029732)
XLA Ops:
  1.6 11.6 %all-to-all-start = ((f32[16,16,294]{2,1,0:T(8,128)}), f32[16,16,294]{2,1,0:T(8,128)}, u32[]{:S(2)}, u32[]{:S(2)}) async-start(f32[16,16,294]{2,1,0:T(8,128)} %broadcast_in_dim.84), calls=%async_computation | async-start | bytes 786432 | tf_op jit(solution)/shard_map/all_to_all | solution.py:17
  13.2 24.9 %all_gather.3 = f32[256,294]{1,0:T(8,128)S(1)} all-gather(f32[16,294]{1,0:T(8,128)S(1)} %pad_maximum_fusion), channel_id=1, replica_groups=mesh['row'=16,'col'=16] {'row'}, dimensions={0}, use_global_device_ids=true | all-gather | bytes 319872 | tf_op jit(solution)/shard_map/all_gather | solution.py:44
  38.5 4.9 %multiply_reduce_fusion = (f32[256,1176]{0,1:T(8,128)S(1)}, f32[256,3,1176]{0,2,1:T(8,128)}) fusion(f32[256,3,49]{0,2,1:T(8,128)S(1)} %dot_general.52, s32[1176]{0:T(1024)S(1)} %get-tuple-element.11, s32[1176]{0:T(1024)S(1)} %get-tuple-element.10), kind=kOutput, calls=%fused_computation.3 | convolution fusion | flops 532856192 | bytes 4976832 | tf_op jit(solution)/shard_map/dot_general | solution.py:68
  44.3 5.3 %fusion.7 = f32[256,1176]{0,1:T(8,128)S(1)} fusion(f32[256,3,1176]{0,2,1:T(8,128)} %get-tuple-element.19, f32[256,3,49]{0,2,1:T(8,128)S(1)} %dot_general.55, s32[1176]{0:T(1024)S(1)} %get-tuple-element.11, s32[1176]{0:T(1024)S(1)} %get-tuple-element.10), kind=kOutput, calls=%fused_computation.18 | convolution fusion | flops 532856192 | bytes 4976832 | tf_op jit(solution)/shard_map/dot_general | solution.py:71
  50.1 1.2 fusion.91
  53.4 4.3 %multiply_reduce_fusion.1 = (f32[144,1176]{1,0:T(8,128)S(1)}, f32[144,3,1176]{2,0,1:T(8,128)}) fusion(s32[1176]{0:T(1024)S(1)} %get-tuple-element.11, s32[1176]{0:T(1024)S(1)} %get-tuple-element.10, f32[144,3,49]{2,1,0:T(4,128)} %dot_general.50), kind=kOutput, calls=%fused_computation.15 | convolution fusion | flops 299857664 | bytes 2803584 | tf_op jit(solution)/shard_map/dot_general | solution.py:68
  58.6 3.7 %fusion.8 = f32[144,1176]{1,0:T(8,128)S(1)} fusion(f32[144,3,1176]{2,0,1:T(8,128)} %get-tuple-element.21, f32[144,3,49]{2,1,0:T(4,128)} %dot_general.62, s32[1176]{0:T(1024)S(1)} %get-tuple-element.11, s32[1176]{0:T(1024)S(1)} %get-tuple-element.10), kind=kOutput, calls=%fused_computation.19 | convolution fusion | flops 299857664 | bytes 2803584 | tf_op jit(solution)/shard_map/dot_general | solution.py:71
  62.9 1.1 fusion.31
  64.0 1.5 %fusion.77 = f32[144,1176]{1,0:T(8,128)S(1)} fusion(f32[144,256]{1,0:T(8,128)S(1)} %reshape.182, f32[144,256]{1,0:T(8,128)S(1)} %fusion.31, f32[256,1176]{0,1:T(8,128)S(1)} %fusion.7, f32[256,1176]{0,1:T(8,128)S(1)} %get-tuple-element.18, f32[1176]{0:T(1024)S(1)} %copy-done.4), kind=kOutput, calls=%fused_computation.95 | convolution fusion | flops 521951232 | bytes 3385440 | tf_op jit(solution)/shard_map/dot_general | solution.py:109
  65.6 1.3 fusion.93
  66.9 1.4 %fusion.6 = f32[144,1176]{1,0:T(8,128)S(1)} fusion(f32[144,1176]{1,0:T(8,128)S(1)} %fusion.77, f32[144,256]{1,0:T(8,128)S(1)} %get-tuple-element.23, f32[256,1176]{0,1:T(8,128)S(1)} %get-tuple-element.18, f32[1176]{0:T(1024)S(1)} %copy-done.4, f32[144,1176]{1,0:T(8,128)S(1)} %get-tuple-element.20, f32[144]{0:T(256)S(1)} %get-tuple-element.22), kind=kOutput, calls=%fused_computation.14 | convolution fusion | flops 522049920 | bytes 3389088 | tf_op jit(solution)/shard_map/dot_general | solution.py:110
  68.7 3.1 %copy.19 = f32[144,3,1176]{2,1,0:T(4,128)} copy(f32[144,3,1176]{2,0,1:T(8,128)S(1)} %broadcast_multiply_fusion.1) | data formatting | bytes 4064256 | tf_op jit(solution)/shard_map/mul | solution.py:83
  71.8 4.4 %reshape.183 = f32[432,1176]{1,0:T(8,128)} reshape(f32[144,3,1176]{2,1,0:T(4,128)} %copy.19) | data formatting | bytes 4064256 | tf_op jit(solution)/shard_map/reshape | solution.py:84
  76.2 3.5 %fusion.58 = f32[432,49]{1,0:T(8,128)S(1)} fusion(f32[432,1176]{1,0:T(8,128)} %reshape.183, s32[1176]{0:T(1024)S(1)} %get-tuple-element.11, s32[1176]{0:T(1024)S(1)} %get-tuple-element.10), kind=kOutput, calls=%fused_computation.70 | convolution fusion | flops 299010944 | bytes 2126208 | tf_op jit(solution)/shard_map/dot_general | solution.py:84
  81.0 9.4 %all-to-all-start.1 = ((f32[16,16,147]{2,1,0:T(8,128)}), f32[16,16,147]{2,1,0:T(8,128)S(1)}, u32[]{:S(2)}, u32[]{:S(2)}) async-start(f32[16,16,147]{2,1,0:T(8,128)} %copy.22), calls=%async_computation.1 | async-start | bytes 524288 | tf_op jit(solution)/shard_map/all_to_all | solution.py:54
  90.5 1.2 fusion.94
  91.7 2.4 %fusion.1 = f32[256,1176]{0,1:T(8,128)S(1)} fusion(f32[144,256]{1,0:T(8,128)S(1)} %get-tuple-element.25, f32[256,1176]{0,1:T(8,128)S(1)} %get-tuple-element.18, f32[256]{0:T(256)S(1)} %get-tuple-element.24, f32[1176]{0:T(1024)S(1)} %copy-done.4, f32[144,1176]{1,0:T(8,128)S(1)} %get-tuple-element.20), kind=kOutput, calls=%fused_computation.8 | convolution fusion | flops 521598336 | bytes 3239008 | tf_op jit(solution)/shard_map/dot_general | solution.py:113
  94.0 2.6 %fusion.2 = f32[256,1176]{0,1:T(8,128)S(1)} fusion(f32[256,1176]{0,1:T(8,128)S(1)} %fusion.1, f32[256,1176]{0,1:T(8,128)S(1)} %get-tuple-element.18, f32[1176]{0:T(1024)S(1)} %copy-done.4, f32[144,256]{1,0:T(8,128)S(1)} %reshape.182, f32[144,256]{1,0:T(8,128)S(1)} %fusion.31, f32[144,1176]{1,0:T(8,128)S(1)} %copy-done.3, f32[144,1176]{1,0:T(8,128)S(1)} %get-tuple-element.20), kind=kOutput, calls=%fused_computation.9 | convolution fusion | flops 523099008 | bytes 5267040 | tf_op jit(solution)/shard_map/dot_general | solution.py:112
  96.6 2.3 %broadcast_multiply_fusion = f32[256,3,1176]{0,2,1:T(8,128)} fusion(f32[256,3,1176]{0,2,1:T(8,128)S(1)} %copy-done, f32[256,1176]{0,1:T(8,128)S(1)} %fusion.2), kind=kLoop, calls=%fused_computation.17 | loop fusion | flops 903168 | bytes 8429568 | tf_op jit(solution)/shard_map/mul | solution.py:83
  98.9 6.4 %copy.24 = f32[256,3,1176]{2,1,0:T(4,128)} copy(f32[256,3,1176]{0,2,1:T(8,128)} %broadcast_multiply_fusion) | data formatting | bytes 7225344 | tf_op jit(solution)/shard_map/mul | solution.py:83
  105.3 7.3 %reshape.185 = f32[768,1176]{1,0:T(8,128)} reshape(f32[256,3,1176]{2,1,0:T(4,128)} %copy.24) | data formatting | bytes 7225344 | tf_op jit(solution)/shard_map/reshape | solution.py:84
  112.6 5.3 %fusion.59 = f32[768,49]{1,0:T(8,128)S(1)} fusion(f32[768,1176]{1,0:T(8,128)} %reshape.185, s32[1176]{0:T(1024)S(1)} %get-tuple-element.11, s32[1176]{0:T(1024)S(1)} %get-tuple-element.10), kind=kOutput, calls=%fused_computation.71 | convolution fusion | flops 531350912 | bytes 3772608 | tf_op jit(solution)/shard_map/dot_general | solution.py:84
  118.7 3.8 %all-to-all-start.2 = ((f32[16,16,147]{2,1,0:T(8,128)}), f32[16,16,147]{2,1,0:T(8,128)S(1)}, u32[]{:S(2)}, u32[]{:S(2)}) async-start(f32[16,16,147]{2,1,0:T(8,128)} %reshape_reshape.9), calls=%async_computation.2 | async-start | bytes 524288 | tf_op jit(solution)/shard_map/all_to_all | solution.py:54
  122.5 7.2 %all-to-all-done.2 = f32[16,16,147]{2,1,0:T(8,128)S(1)} async-done(((f32[16,16,147]{2,1,0:T(8,128)}), f32[16,16,147]{2,1,0:T(8,128)S(1)}, u32[]{:S(2)}, u32[]{:S(2)}) %all-to-all-start.2) | async-done | bytes 150560 | tf_op jit(solution)/shard_map/all_to_all | solution.py:54
  (45 shorter events, 9.9 us)
Async XLA Ops:
  0.0 38.1 %copy-start.5 = (s32[2,1176]{1,0:T(2,128)S(1)}, s32[2,1176]{1,0:T(2,128)}, u32[]{:S(2)}) copy-start(s32[2,1176]{1,0:T(2,128)} %param.8) | copy-start | bytes 28228
  1.6 48.5 %all-to-all-start = ((f32[16,16,294]{2,1,0:T(8,128)}), f32[16,16,294]{2,1,0:T(8,128)}, u32[]{:S(2)}, u32[]{:S(2)}) async-start(f32[16,16,294]{2,1,0:T(8,128)} %broadcast_in_dim.84), calls=%async_computation | async-start | bytes 786432 | tf_op jit(solution)/shard_map/all_to_all | solution.py:17
  44.3 5.3 %copy-start.4 = (f32[1176]{0:T(1024)S(1)}, f32[1176]{0:T(1024)}, u32[]{:S(2)}) copy-start(f32[1176]{0:T(1024)} %param.9) | copy-start | bytes 14116
  62.4 1.7 %copy-start.2 = (f32[144,1176]{1,0:T(8,128)}, f32[144,1176]{1,0:T(8,128)S(1)}, u32[]{:S(2)}) copy-start(f32[144,1176]{1,0:T(8,128)S(1)} %fusion.8) | copy-start | bytes 2032132
  66.8 1.6 %copy-start.1 = (f32[144,3,1176]{2,0,1:T(8,128)S(1)}, f32[144,3,1176]{2,0,1:T(8,128)}, u32[]{:S(2)}) copy-start(f32[144,3,1176]{2,0,1:T(8,128)} %get-tuple-element.21) | copy-start | bytes 6096388
  79.7 10.7 %copy-start.3 = (f32[144,1176]{1,0:T(8,128)S(1)}, f32[144,1176]{1,0:T(8,128)}, u32[]{:S(2)}) copy-start(f32[144,1176]{1,0:T(8,128)} %copy-done.2) | copy-start | bytes 2032132
  81.0 37.7 %all-to-all-start.1 = ((f32[16,16,147]{2,1,0:T(8,128)}), f32[16,16,147]{2,1,0:T(8,128)S(1)}, u32[]{:S(2)}, u32[]{:S(2)}) async-start(f32[16,16,147]{2,1,0:T(8,128)} %copy.22), calls=%async_computation.1 | async-start | bytes 524288 | tf_op jit(solution)/shard_map/all_to_all | solution.py:54
  94.0 2.6 %copy-start = (f32[256,3,1176]{0,2,1:T(8,128)S(1)}, f32[256,3,1176]{0,2,1:T(8,128)}, u32[]{:S(2)}) copy-start(f32[256,3,1176]{0,2,1:T(8,128)} %get-tuple-element.19) | copy-start | bytes 10838020
  118.7 11.0 %all-to-all-start.2 = ((f32[16,16,147]{2,1,0:T(8,128)}), f32[16,16,147]{2,1,0:T(8,128)S(1)}, u32[]{:S(2)}, u32[]{:S(2)}) async-start(f32[16,16,147]{2,1,0:T(8,128)} %reshape_reshape.9), calls=%async_computation.2 | async-start | bytes 524288 | tf_op jit(solution)/shard_map/all_to_all | solution.py:54
where the time goes:
time: 131 us; the launch traced here: 130 us
  matrix products  38.9 us (30%)
  local copies, waits for them, and re-layouts  29.1 us (22%)
  blocking collectives  24.9 us (19%)
  starting transfers between devices  24.8 us (19%)
  waiting for transfers between devices  7.21 us (6%)
  other arithmetic  5.23 us (4%)
    all_gather x1, blocking collectives, sent_together_2(): lax.all_gather(both, axis, axis=dim, tiled=True)  24.9 us
    all_to_all x2, starting transfers between devices, sum_at_owner(): lax.all_to_all(parts, axis, split_axis=0, concat_axis=0, tiled=True)  13.2 us
    reshape x2, local copies, waits for them, and re-layouts, pull_back(): terms.reshape(count * 3, -1)  11.7 us
    all_to_all x1, starting transfers between devices, from_everyone(): return lax.all_to_all(copies, axis, split_axis=0, concat_axis=0, tiled=True)  11.6 us
    mul x2, local copies, waits for them, and re-layouts, pull_back(): terms = -(weights * grads)[:, None, :] * spans  9.48 us
    dot_general x2, matrix products, geometry_terms(): jnp.dot(positions.reshape(count * 3, atoms), onehot, precision=highest)  9.27 us
    dot_general x2, matrix products, geometry_terms(): jnp.dot(coefficients.reshape(count * 3, atoms), onehot, precision=highest)  9.03 us
    dot_general x2, matrix products, pull_back(): jnp.dot(terms.reshape(count * 3, -1), onehot.T, precision=highest)  8.8 us
  transfers between devices with their start and end apart: 3, of which 1 were waited for; matrix products, arithmetic and copies ran while one was open for 31% of the time, Pallas kernels for 0%

commit v1 on v0

v1 whole, which is shorter than its diff:
```python
import math

import jax
import jax.numpy as jnp
from jax import lax
from jax.experimental import pallas as pl
from jax.experimental.pallas import tpu as pltpu
from jax.sharding import PartitionSpec as P

ATOMS = 49
HALF = 24
BLOCK = 56
ROWS = HALF * BLOCK
WRAP = 80
CART = 3 * ATOMS
LANES = 128

length_scale = 2.0
decay_rate = math.sqrt(5.0) / length_scale
outer_factor = decay_rate * decay_rate / 3.0
radial_factor = decay_rate * decay_rate
f32 = jnp.float32
bf16 = jnp.bfloat16


def halves(value):
    high = value.astype(bf16)
    return high, (value - high.astype(f32)).astype(bf16)


def dot_nt(a, b):
    return lax.dot_general(a, b, (((1,), (1,)), ((), ())), preferred_element_type=f32)


def dot_nn(a, b):
    return lax.dot_general(a, b, (((1,), (0,)), ((), ())), preferred_element_type=f32)


def pack_kernel(p_ref, c_ref, rows_ref, cols_ref):
    half = p_ref.shape[0] // 2
    p, c = p_ref[...], c_ref[...]
    for n in range(rows_ref.shape[0]):
        rows_ref[n, :, 0:CART] = p[:half]
        rows_ref[n, :, CART : 2 * CART] = p[half:]
    for n in range(cols_ref.shape[0]):
        cols_ref[n, :, 0:CART] = p[:half]
        cols_ref[n, :, CART : 2 * CART] = p[half:]
        cols_ref[n, :, 2 * CART : 3 * CART] = c[:half]
        cols_ref[n, :, 3 * CART : 4 * CART] = c[half:]


def scale_kernel(pairs_ref, scale_ref, out_ref):
    low, high = pairs_ref[0:1, :], pairs_ref[1:2, :]
    apart = high - low
    near = apart <= HALF
    shift = jnp.where(near, apart, ATOMS - apart) - 1
    start = jnp.where(near, low, high)
    count = low.shape[1]
    atom_ids = lax.broadcasted_iota(jnp.int32, (64, count), 0)
    shift_ids = lax.broadcasted_iota(jnp.int32, (32, count), 0)
    at_atom = jnp.where(atom_ids == start, 1.0, 0.0).astype(bf16)
    scaled = jnp.where(shift_ids == shift, scale_ref[...], 0.0)
    top = scaled.astype(bf16)
    rest = scaled - top.astype(f32)
    middle = rest.astype(bf16)
    bottom = (rest - middle.astype(f32)).astype(bf16)
    table = dot_nt(at_atom, top) + dot_nt(at_atom, middle) + dot_nt(at_atom, bottom)
    for d in range(HALF):
        out_ref[d * BLOCK : (d + 1) * BLOCK, :] = jnp.broadcast_to(
            table[0:BLOCK, d : d + 1], (BLOCK, LANES)
        )


def wrap_rows(flat_ref, start, wrapped_ref, *at):
    for k in range(3):
        base = start + k * ATOMS
        wrapped_ref[(*at, k, slice(0, ATOMS), slice(None))] = flat_ref[base : base + ATOMS, :]
        wrapped_ref[(*at, k, slice(ATOMS, WRAP), slice(None))] = flat_ref[
            base : base + WRAP - ATOMS, :
        ]


def spans_of(wrapped_ref, at, d):
    return [
        wrapped_ref[(*at, k, slice(0, BLOCK), slice(None))]
        - wrapped_ref[(*at, k, slice(d, d + BLOCK), slice(None))]
        for k in range(3)
    ]


def fold8(value):
    total = value[0:8]
    for n in range(1, value.shape[0] // 8):
        total = total + value[8 * n : 8 * n + 8]
    return total


def apply_kernel(
    rows_ref, cols_ref, scale_ref, out_ref,
    flat_rows, flat_cols, rows_w, cols_p, cols_c, pair_hi, pair_lo, row_x, row_weight,
    rowx_hi, rowx_lo, grads, back, flat_out,
):
    flat_cols[...] = cols_ref[...].T
    flat_rows[...] = rows_ref[...].T
    for t in range(2):
        wrap_rows(flat_cols, t * CART, cols_p, t)
        wrap_rows(flat_cols, (2 + t) * CART, cols_c, t)
        wrap_rows(flat_rows, t * CART, rows_w, t)

    pad_one = (lax.broadcasted_iota(jnp.int32, (2 * BLOCK, LANES), 0) == ATOMS).astype(f32)
    col_sq, col_xu = [], []
    for t in range(2):
        sq, xu = jnp.zeros((8, LANES), f32), jnp.zeros((8, LANES), f32)
        lanes_x = slice(t * LANES, (t + 1) * LANES)
        lanes_u = slice((2 + t) * LANES, (3 + t) * LANES)
        for pair in range(HALF // 2):
            xs, us = [], []
            for d in (2 * pair + 1, 2 * pair + 2):
                scale = scale_ref[(d - 1) * BLOCK : d * BLOCK, :]
                spans = spans_of(cols_p, (t,), d)
                moves = spans_of(cols_c, (t,), d)
                inverse = lax.rsqrt(spans[0] * spans[0] + spans[1] * spans[1] + spans[2] * spans[2])
                along = spans[0] * moves[0] + spans[1] * moves[1] + spans[2] * moves[2]
                x = scale * inverse
                u = -(x * inverse * inverse) * along
                xu = xu + fold8(x * u)
                xs.append(x)
                us.append(u)
            at = slice(pair * 2 * BLOCK, (pair + 1) * 2 * BLOCK)
            x, u = jnp.concatenate(xs, 0), jnp.concatenate(us, 0)
            high = x.astype(bf16)
            rest = x - high.astype(f32)
            sq = sq + fold8(x * x)
            pair_lo[at, lanes_x] = rest.astype(bf16)
            pair_hi[at, lanes_x] = (x + pad_one).astype(bf16) if pair == 0 else high
            pair_hi[at, lanes_u], pair_lo[at, lanes_u] = halves(u)
        col_sq.append(jnp.sum(sq, axis=0, keepdims=True))
        col_xu.append(jnp.sum(xu, axis=0, keepdims=True))

    row_sq = []
    for t in range(2):
        for d in range(1, HALF + 1):
            at = slice((d - 1) * BLOCK, d * BLOCK)
            spans = spans_of(rows_w, (t,), d)
            inverse = lax.rsqrt(spans[0] * spans[0] + spans[1] * spans[1] + spans[2] * spans[2])
            x = scale_ref[at, :] * inverse
            row_x[t, at, :] = x
            row_weight[t, at, :] = x * inverse * inverse
        sq = 0.0
        for start in range(0, ROWS, LANES):
            stop = min(start + LANES, ROWS)
            turned = row_x[t, start:stop, :].T
            high = turned.astype(bf16)
            rest = turned - high.astype(f32)
            at = slice(t * LANES, (t + 1) * LANES)
            rowx_hi[at, start:stop] = high
            rowx_lo[at, start:stop] = rest.astype(bf16)
            sq = sq + jnp.sum(turned * turned, axis=1, keepdims=True)
        row_sq.append(sq)

    high, low = rowx_hi[...], rowx_lo[...]
    products = (
        dot_nn(high, pair_hi[...]) + dot_nn(high, pair_lo[...]) + dot_nn(low, pair_hi[...])
    )
    count = 2 * LANES
    gram = products[:, :count] + dot_nn(low, pair_lo[:, :count])
    sq_dist = jnp.concatenate(row_sq, axis=0) + jnp.concatenate(col_sq, axis=1) - 2.0 * gram
    radius = jnp.sqrt(jnp.maximum(sq_dist, 0.0))
    envelope = outer_factor * jnp.exp(-decay_rate * radius)
    direct = envelope * (1.0 + decay_rate * radius)
    bent = (radial_factor * envelope) * (products[:, count:] - jnp.concatenate(col_xu, axis=1))
    high, low = halves(jnp.concatenate([bent, direct], axis=1))
    grads[...] = (
        dot_nt(pair_hi[...], high) + dot_nt(pair_lo[...], high) + dot_nt(pair_hi[...], low)
    )

    for t in range(2):
        lanes = slice(t * LANES, (t + 1) * LANES)
        bend = grads[ATOMS : ATOMS + 1, lanes]
        here = [jnp.zeros((BLOCK, LANES), f32) for _ in range(3)]
        back[...] = jnp.zeros_like(back)
        for d in range(1, HALF + 1):
            at = slice((d - 1) * BLOCK, d * BLOCK)
            pull = row_weight[t, at, :] * (grads[at, lanes] - bend * row_x[t, at, :])
            spans = spans_of(rows_w, (t,), d)
            for k in range(3):
                term = pull * spans[k]
                here[k] = here[k] + term
                back[k, d : d + BLOCK, :] = back[k, d : d + BLOCK, :] + term
        for k in range(3):
            back[k, 0:BLOCK, :] = back[k, 0:BLOCK, :] - here[k]
            back[k, 0:HALF, :] = back[k, 0:HALF, :] + back[k, ATOMS : ATOMS + HALF, :]
            base = t * CART + k * ATOMS
            flat_out[base : base + ATOMS, :] = back[k, 0:ATOMS, :]
    out_ref[...] = flat_out[...].T


def vmem(count):
    return [pl.BlockSpec(memory_space=pltpu.VMEM)] * count


def tile_apply(rows, cols, scale):
    return pl.pallas_call(
        apply_kernel,
        out_shape=jax.ShapeDtypeStruct(rows.shape, f32),
        in_specs=vmem(3),
        out_specs=vmem(1)[0],
        scratch_shapes=[
            pltpu.VMEM((2 * CART, LANES), f32),
            pltpu.VMEM((4 * CART, LANES), f32),
            pltpu.VMEM((2, 3, WRAP, LANES), f32),
            pltpu.VMEM((2, 3, WRAP, LANES), f32),
            pltpu.VMEM((2, 3, WRAP, LANES), f32),
            pltpu.VMEM((ROWS, 4 * LANES), bf16),
            pltpu.VMEM((ROWS, 4 * LANES), bf16),
            pltpu.VMEM((2, ROWS, LANES), f32),
            pltpu.VMEM((2, ROWS, LANES), f32),
            pltpu.VMEM((2 * LANES, ROWS), bf16),
            pltpu.VMEM((2 * LANES, ROWS), bf16),
            pltpu.VMEM((ROWS, 2 * LANES), f32),
            pltpu.VMEM((3, WRAP, LANES), f32),
            pltpu.VMEM((2 * CART, LANES), f32),
        ],
        compiler_params=pltpu.CompilerParams(vmem_limit_bytes=40 * 1024 * 1024),
        cost_estimate=pl.CostEstimate(flops=2_000_000_000, bytes_accessed=2_000_000, transcendentals=1_000_000),
    )(rows, cols, scale)


def scale_table(atom_pairs, pair_scale):
    return pl.pallas_call(
        scale_kernel,
        out_shape=jax.ShapeDtypeStruct((ROWS, LANES), f32),
        in_specs=vmem(2),
        out_specs=vmem(1)[0],
        cost_estimate=pl.CostEstimate(flops=20_000_000, bytes_accessed=700_000, transcendentals=0),
    )(atom_pairs, pair_scale.reshape(1, -1))


def pack(positions, coefficients, row_peers, col_peers):
    half = positions.shape[0] // 2
    return pl.pallas_call(
        pack_kernel,
        out_shape=(
            jax.ShapeDtypeStruct((row_peers, half, 2 * CART), f32),
            jax.ShapeDtypeStruct((col_peers, half, 4 * CART), f32),
        ),
        in_specs=vmem(2),
        out_specs=tuple(vmem(2)),
        cost_estimate=pl.CostEstimate(flops=0, bytes_accessed=400_000, transcendentals=0),
    )(positions, coefficients)


def exchange(value, axis, groups=None):
    return lax.all_to_all(value, axis, split_axis=0, concat_axis=0, tiled=True, axis_index_groups=groups)


def on_device(positions, coefficients, atom_pairs, pair_scale):
    row_count, col_count = lax.axis_size("row"), lax.axis_size("col")
    half = positions.shape[0] // 2
    to_rows, to_cols = pack(positions, coefficients, col_count, row_count // 2)
    scale = scale_table(atom_pairs, pair_scale)
    rows = exchange(to_rows, "col").reshape(-1, 2 * CART)
    same_core = [list(range(core, row_count, 2)) for core in range(2)]
    one_chip = [[n, n + 1] for n in range(0, row_count, 2)]
    cols = exchange(to_cols, "row", same_core).reshape(-1, 4 * CART)
    cols = lax.all_gather(cols, "row", axis=0, tiled=True, axis_index_groups=one_chip)
    partial = tile_apply(rows, cols, scale)
    arrived = exchange(partial.reshape(col_count, half, 2 * CART), "col")
    total = arrived.sum(axis=0)
    return jnp.concatenate([total[:, :CART], total[:, CART:]], axis=0)


def solution(mesh):
    in_specs = (P(("row", "col"), None), P(("row", "col"), None), P(), P())
    out_specs = P(("row", "col"), None)
    return jax.shard_map(
        on_device, mesh=mesh, in_specs=in_specs, out_specs=out_specs, check_vma=False
    )
```

time: 131 us -> 59.6 us (0.45)
  matrix products: 38.9 us -> 0 us
  local copies, waits for them, and re-layouts: 29.1 us -> 1.77 us
  starting transfers between devices: 24.8 us -> 9.98 us
  Pallas kernels: 0 us -> 10.6 us
  blocking collectives: 24.9 us -> 32.7 us
  other arithmetic: 5.23 us -> 0.64 us
  waiting for transfers between devices: 7.21 us -> 3.33 us
    dot_general x14 -> x0, matrix products: 38.9 us -> none  [the longest x2 9.27 us: geometry_terms(): jnp.dot(positions.reshape(count * 3, atoms), onehot, precision=highest)]
    all_to_all x0 -> x2, blocking collectives: none -> 28.7 us  [exchange(): lax.all_to_all(value, axis, split_axis=0, concat_axis=0, tiled=True, axis...]
    all_gather x1, blocking collectives: 24.9 us -> 4 us  [on_device(): lax.all_gather(cols, 'row', axis=0, tiled=True, axis_index_groups=one_chip)]
    all_to_all x3 -> x1, starting transfers between devices: 24.8 us -> 9.98 us  [exchange(): lax.all_to_all(value, axis, split_axis=0, concat_axis=0, tiled=True, axis...]
    reshape x3 -> x1, local copies, waits for them, and re-layouts: 12.2 us -> 0.6 us  [scale_table(): pair_scale.reshape(1, -1)]
    pallas_call x0 -> x3, Pallas kernels: none -> 10.6 us  [the longest x1 6.86 us: tile_apply(): pl.pallas_call(apply_kernel, out_shape=jax.ShapeDtypeStruct(rows.shape, f...]
    mul x2 -> x0, local copies, waits for them, and re-layouts: 9.48 us -> none  [pull_back(): terms = -(weights * grads)[:, None, :] * spans]
    all_to_all x3 -> x1, waiting for transfers between devices: 7.21 us -> 3.33 us  [exchange(): lax.all_to_all(value, axis, split_axis=0, concat_axis=0, tiled=True, axis...]
  transfers between devices with their start and end apart: 3 -> 1, of which waited for: 1 -> 1; matrix products, arithmetic and copies ran while one was open for 31% -> 1% of each run, Pallas kernels for 0% -> 4%
where the time goes in v1:
time: 59.6 us; the launch traced here: 59 us
  blocking collectives  32.7 us (55%)
  Pallas kernels  10.6 us (18%)
  starting transfers between devices  9.98 us (17%)
  waiting for transfers between devices  3.33 us (6%)
  local copies, waits for them, and re-layouts  1.77 us (3%)
  other arithmetic  0.64 us (1%)
    all_to_all x2, blocking collectives, exchange(): lax.all_to_all(value, axis, split_axis=0, concat_axis=0, tiled=True, axis...  28.7 us
    all_to_all x1, starting transfers between devices, exchange(): lax.all_to_all(value, axis, split_axis=0, concat_axis=0, tiled=True, axis...  9.98 us
    pallas_call x1, Pallas kernels, tile_apply(): pl.pallas_call(apply_kernel, out_shape=jax.ShapeDtypeStruct(rows.shape, f...  6.86 us
    all_gather x1, blocking collectives, on_device(): lax.all_gather(cols, 'row', axis=0, tiled=True, axis_index_groups=one_chip)  4 us
    all_to_all x1, waiting for transfers between devices, exchange(): lax.all_to_all(value, axis, split_axis=0, concat_axis=0, tiled=True, axis...  3.33 us
    pallas_call x1, Pallas kernels, scale_table(): pl.pallas_call(scale_kernel, out_shape=jax.ShapeDtypeStruct((ROWS, LANES)...  2.15 us
    pallas_call x1, Pallas kernels, pack(): pl.pallas_call(pack_kernel, out_shape=(jax.ShapeDtypeStruct((row_peers, h...  1.55 us
  transfers between devices with their start and end apart: 1, of which 1 were waited for; matrix products, arithmetic and copies ran while one was open for 1% of the time, Pallas kernels for 4%

profile of v1, /device:TPU:1, one launch (start us, length us, event | category | flops | bytes accessed | tf_op | source)
XLA Modules:
  0.0 59.0 jit_solution(9893118308002087276)
XLA Ops:
  0.0 1.5 %shard_map.46 = (f32[16,8,294]{2,1,0:T(8,128)}, f32[8,8,588]{2,1,0:T(8,128)}) custom-call(f32[16,147]{1,0:T(8,128)} %p_ref.1, f32[16,147]{1,0:T(8,128)} %c_ref.1), custom_call_target="tpu_custom_call" | custom-call | bytes 400000 | tf_op jit(solution)/shard_map/pallas_call | solution.py:241
  1.6 12.1 %all_to_all.15 = f32[8,8,588]{2,1,0:T(8,128)S(1)} all-to-all(f32[8,8,588]{2,1,0:T(8,128)} %get-tuple-element.8), channel_id=1, replica_groups={{0,32,64,96,128,160,192,224},{16,48,80,112,144,176,208,240},{1,33,65,97..., dimensions={0} | all-to-all | bytes 301056 | tf_op jit(solution)/shard_map/all_to_all | solution.py:254
  13.6 0.0 copy-start.1
  13.6 10.0 %all-to-all-start = ((f32[16,8,294]{2,1,0:T(8,128)}), f32[16,8,294]{2,1,0:T(8,128)S(1)}, u32[]{:S(2)}, u32[]{:S(2)}) async-start(f32[16,8,294]{2,1,0:T(8,128)} %get-tuple-element.7), calls=%async_computation | async-start | bytes 393216 | tf_op jit(solution)/shard_map/all_to_all | solution.py:254
  23.6 0.0 copy-done.1
  23.6 0.6 %reshape.14.scale_ref = f32[1,1176]{1,0:T(1,128)} reshape(f32[1176]{0:T(1024)S(1)} %copy-done.1) | data formatting | bytes 9408 | tf_op jit(solution)/shard_map/reshape | solution.py:236
  24.2 2.1 %shard_map.47.scale_ref = f32[1344,128]{1,0:T(8,128)} custom-call(s32[2,1176]{1,0:T(2,128)} %pairs_ref.1, f32[1,1176]{1,0:T(1,128)} %reshape.14.scale_ref), custom_call_target="tpu_custom_call" | custom-call | flops 20000000 | bytes 700000 | tf_op jit(solution)/shard_map/pallas_call | solution.py:230
  26.4 4.0 %all_gather.3.cols_ref = f32[128,588]{1,0:T(8,128)S(1)} all-gather(f32[64,588]{1,0:T(8,128)S(1)} %bitcast.5), channel_id=1, replica_groups={{0,16},{32,48},{64,80},{96,112},{128,144},{160,176},{192,208},{224,240}..., dimensions={0}, use_global_device_ids=true | all-gather | bytes 451584 | tf_op jit(solution)/shard_map/all_gather | solution.py:266
  30.4 3.3 %all-to-all-done = f32[16,8,294]{2,1,0:T(8,128)S(1)} async-done(((f32[16,8,294]{2,1,0:T(8,128)}), f32[16,8,294]{2,1,0:T(8,128)S(1)}, u32[]{:S(2)}, u32[]{:S(2)}) %all-to-all-start) | async-done | bytes 150560 | tf_op jit(solution)/shard_map/all_to_all | solution.py:254
  33.7 0.0 copy-start
  33.7 1.1 %copy-done = f32[1344,128]{1,0:T(8,128)S(1)} copy-done((f32[1344,128]{1,0:T(8,128)S(1)}, f32[1344,128]{1,0:T(8,128)}, u32[]{:S(2)}) %copy-start) | copy-done | bytes 688152
  34.8 6.9 %shard_map.48 = f32[128,294]{1,0:T(8,128)S(1)} custom-call(f32[128,294]{1,0:T(8,128)S(1)} %bitcast.3, f32[128,588]{1,0:T(8,128)S(1)} %all_gather.3.cols_ref, f32[1344,128]{1,0:T(8,128)S(1)} %copy-done), custom_call_target="tpu_custom_call" | custom-call | flops 2000000000 | bytes 2000000 | tf_op jit(solution)/shard_map/pallas_call | solution.py:203
  41.7 16.6 %all_to_all.16 = f32[16,8,294]{2,1,0:T(8,128)S(1)} all-to-all(f32[16,8,294]{2,1,0:T(8,128)S(1)} %bitcast.4), channel_id=1, replica_groups=mesh['row'=16,'col'=16] {'col'}, dimensions={0} | all-to-all | bytes 301056 | tf_op jit(solution)/shard_map/all_to_all | solution.py:254
  58.3 0.1 fusion
  58.4 0.6 %pad_maximum_fusion = f32[16,147]{1,0:T(8,128)} fusion(f32[8,147]{1,0:T(8,128)S(1)} %get-tuple-element.10, f32[8,147]{1,0:T(8,128)S(1)} %get-tuple-element.9), kind=kLoop, calls=%fused_computation | loop fusion | flops 2352 | bytes 18816 | tf_op jit(solution)/shard_map/concatenate | solution.py:270
  (1 shorter events, 0.0 us)
Async XLA Ops:
  13.6 10.0 %copy-start.1 = (f32[1176]{0:T(1024)S(1)}, f32[1176]{0:T(1024)}, u32[]{:S(2)}) copy-start(f32[1176]{0:T(1024)} %param.7) | copy-start | bytes 14116
  13.6 20.1 %all-to-all-start = ((f32[16,8,294]{2,1,0:T(8,128)}), f32[16,8,294]{2,1,0:T(8,128)S(1)}, u32[]{:S(2)}, u32[]{:S(2)}) async-start(f32[16,8,294]{2,1,0:T(8,128)} %get-tuple-element.7), calls=%async_computation | async-start | bytes 393216 | tf_op jit(solution)/shard_map/all_to_all | solution.py:254
  33.7 1.1 %copy-start = (f32[1344,128]{1,0:T(8,128)S(1)}, f32[1344,128]{1,0:T(8,128)}, u32[]{:S(2)}) copy-start(f32[1344,128]{1,0:T(8,128)} %shard_map.47.scale_ref) | copy-start | bytes 2064388

commit v2 on v1

--- a/solution.py
+++ b/solution.py
@@ -36,20 +36,7 @@
     return lax.dot_general(a, b, (((1,), (0,)), ((), ())), preferred_element_type=f32)
 
 
-def pack_kernel(p_ref, c_ref, rows_ref, cols_ref):
-    half = p_ref.shape[0] // 2
-    p, c = p_ref[...], c_ref[...]
-    for n in range(rows_ref.shape[0]):
-        rows_ref[n, :, 0:CART] = p[:half]
-        rows_ref[n, :, CART : 2 * CART] = p[half:]
-    for n in range(cols_ref.shape[0]):
-        cols_ref[n, :, 0:CART] = p[:half]
-        cols_ref[n, :, CART : 2 * CART] = p[half:]
-        cols_ref[n, :, 2 * CART : 3 * CART] = c[:half]
-        cols_ref[n, :, 3 * CART : 4 * CART] = c[half:]
-
-
-def scale_kernel(pairs_ref, scale_ref, out_ref):
+def spread_scale(pairs_ref, scale_ref, out_ref):
     low, high = pairs_ref[0:1, :], pairs_ref[1:2, :]
     apart = high - low
     near = apart <= HALF
@@ -95,17 +82,44 @@
     return total
 
 
+def rows_kernel(
+    rows_ref, pairs_ref, pair_scale_ref,
+    scale_ref, rows_w, row_x, row_weight, rowx_hi, rowx_lo, row_sq,
+    flat_rows,
+):
+    spread_scale(pairs_ref, pair_scale_ref, scale_ref)
+    flat_rows[...] = rows_ref[...].T
+    for t in range(2):
+        wrap_rows(flat_rows, t * CART, rows_w, t)
+    for t in range(2):
+        for d in range(1, HALF + 1):
+            at = slice((d - 1) * BLOCK, d * BLOCK)
+            spans = spans_of(rows_w, (t,), d)
+            inverse = lax.rsqrt(spans[0] * spans[0] + spans[1] * spans[1] + spans[2] * spans[2])
+            x = scale_ref[at, :] * inverse
+            row_x[t, at, :] = x
+            row_weight[t, at, :] = x * inverse * inverse
+        sq = 0.0
+        for start in range(0, ROWS, LANES):
+            stop = min(start + LANES, ROWS)
+            turned = row_x[t, start:stop, :].T
+            high = turned.astype(bf16)
+            rest = turned - high.astype(f32)
+            at = slice(t * LANES, (t + 1) * LANES)
+            rowx_hi[at, start:stop] = high
+            rowx_lo[at, start:stop] = rest.astype(bf16)
+            sq = sq + jnp.sum(turned * turned, axis=1, keepdims=True)
+        row_sq[t * LANES : (t + 1) * LANES, :] = jnp.broadcast_to(sq, (LANES, LANES))
+
+
 def apply_kernel(
-    rows_ref, cols_ref, scale_ref, out_ref,
-    flat_rows, flat_cols, rows_w, cols_p, cols_c, pair_hi, pair_lo, row_x, row_weight,
-    rowx_hi, rowx_lo, grads, back, flat_out,
+    cols_ref, scale_ref, rows_w, row_x, row_weight, rowx_hi, rowx_lo, row_sq, out_ref,
+    flat_cols, cols_p, cols_c, pair_hi, pair_lo, grads, back, flat_out,
 ):
     flat_cols[...] = cols_ref[...].T
-    flat_rows[...] = rows_ref[...].T
     for t in range(2):
         wrap_rows(flat_cols, t * CART, cols_p, t)
         wrap_rows(flat_cols, (2 + t) * CART, cols_c, t)
-        wrap_rows(flat_rows, t * CART, rows_w, t)
 
     pad_one = (lax.broadcasted_iota(jnp.int32, (2 * BLOCK, LANES), 0) == ATOMS).astype(f32)
     col_sq, col_xu = [], []
@@ -137,34 +151,13 @@
         col_sq.append(jnp.sum(sq, axis=0, keepdims=True))
         col_xu.append(jnp.sum(xu, axis=0, keepdims=True))
 
-    row_sq = []
-    for t in range(2):
-        for d in range(1, HALF + 1):
-            at = slice((d - 1) * BLOCK, d * BLOCK)
-            spans = spans_of(rows_w, (t,), d)
-            inverse = lax.rsqrt(spans[0] * spans[0] + spans[1] * spans[1] + spans[2] * spans[2])
-            x = scale_ref[at, :] * inverse
-            row_x[t, at, :] = x
-            row_weight[t, at, :] = x * inverse * inverse
-        sq = 0.0
-        for start in range(0, ROWS, LANES):
-            stop = min(start + LANES, ROWS)
-            turned = row_x[t, start:stop, :].T
-            high = turned.astype(bf16)
-            rest = turned - high.astype(f32)
-            at = slice(t * LANES, (t + 1) * LANES)
-            rowx_hi[at, start:stop] = high
-            rowx_lo[at, start:stop] = rest.astype(bf16)
-            sq = sq + jnp.sum(turned * turned, axis=1, keepdims=True)
-        row_sq.append(sq)
-
     high, low = rowx_hi[...], rowx_lo[...]
     products = (
         dot_nn(high, pair_hi[...]) + dot_nn(high, pair_lo[...]) + dot_nn(low, pair_hi[...])
     )
     count = 2 * LANES
     gram = products[:, :count] + dot_nn(low, pair_lo[:, :count])
-    sq_dist = jnp.concatenate(row_sq, axis=0) + jnp.concatenate(col_sq, axis=1) - 2.0 * gram
+    sq_dist = row_sq[:, 0:1] + jnp.concatenate(col_sq, axis=1) - 2.0 * gram
     radius = jnp.sqrt(jnp.maximum(sq_dist, 0.0))
     envelope = outer_factor * jnp.exp(-decay_rate * radius)
     direct = envelope * (1.0 + decay_rate * radius)
@@ -199,73 +192,79 @@
     return [pl.BlockSpec(memory_space=pltpu.VMEM)] * count
 
 
-def tile_apply(rows, cols, scale):
+def shape(*dims, kind=f32):
+    return jax.ShapeDtypeStruct(dims, kind)
+
+
+params = pltpu.CompilerParams(vmem_limit_bytes=20 * 1024 * 1024)
+
+
+def row_terms(rows, atom_pairs, pair_scale):
+    return pl.pallas_call(
+        rows_kernel,
+        out_shape=(
+            shape(ROWS, LANES),
+            shape(2, 3, WRAP, LANES),
+            shape(2, ROWS, LANES),
+            shape(2, ROWS, LANES),
+            shape(2 * LANES, ROWS, kind=bf16),
+            shape(2 * LANES, ROWS, kind=bf16),
+            shape(2 * LANES, LANES),
+        ),
+        in_specs=vmem(3),
+        out_specs=tuple(vmem(7)),
+        scratch_shapes=[pltpu.VMEM((2 * CART, LANES), f32)],
+        compiler_params=params,
+        cost_estimate=pl.CostEstimate(
+            flops=40_000_000, bytes_accessed=6_000_000, transcendentals=300_000
+        ),
+    )(rows, atom_pairs, pair_scale.reshape(1, -1))
+
+
+def tile_apply(cols, terms):
     return pl.pallas_call(
         apply_kernel,
-        out_shape=jax.ShapeDtypeStruct(rows.shape, f32),
-        in_specs=vmem(3),
+        out_shape=shape(LANES, 2 * CART),
+        in_specs=vmem(1 + len(terms)),
         out_specs=vmem(1)[0],
         scratch_shapes=[
-            pltpu.VMEM((2 * CART, LANES), f32),
             pltpu.VMEM((4 * CART, LANES), f32),
-            pltpu.VMEM((2, 3, WRAP, LANES), f32),
             pltpu.VMEM((2, 3, WRAP, LANES), f32),
             pltpu.VMEM((2, 3, WRAP, LANES), f32),
             pltpu.VMEM((ROWS, 4 * LANES), bf16),
             pltpu.VMEM((ROWS, 4 * LANES), bf16),
-            pltpu.VMEM((2, ROWS, LANES), f32),
-            pltpu.VMEM((2, ROWS, LANES), f32),
-            pltpu.VMEM((2 * LANES, ROWS), bf16),
-            pltpu.VMEM((2 * LANES, ROWS), bf16),
             pltpu.VMEM((ROWS, 2 * LANES), f32),
             pltpu.VMEM((3, WRAP, LANES), f32),
             pltpu.VMEM((2 * CART, LANES), f32),
         ],
-        compiler_params=pltpu.CompilerParams(vmem_limit_bytes=40 * 1024 * 1024),
-        cost_estimate=pl.CostEstimate(flops=2_000_000_000, bytes_accessed=2_000_000, transcendentals=1_000_000),
-    )(rows, cols, scale)
-
-
-def scale_table(atom_pairs, pair_scale):
-    return pl.pallas_call(
-        scale_kernel,
-        out_shape=jax.ShapeDtypeStruct((ROWS, LANES), f32),
-        in_specs=vmem(2),
-        out_specs=vmem(1)[0],
-        cost_estimate=pl.CostEstimate(flops=20_000_000, bytes_accessed=700_000, transcendentals=0),
-    )(atom_pairs, pair_scale.reshape(1, -1))
-
-
-def pack(positions, coefficients, row_peers, col_peers):
-    half = positions.shape[0] // 2
-    return pl.pallas_call(
-        pack_kernel,
-        out_shape=(
-            jax.ShapeDtypeStruct((row_peers, half, 2 * CART), f32),
-            jax.ShapeDtypeStruct((col_peers, half, 4 * CART), f32),
+        compiler_params=params,
+        cost_estimate=pl.CostEstimate(
+            flops=2_000_000_000, bytes_accessed=6_000_000, transcendentals=500_000
         ),
-        in_specs=vmem(2),
-        out_specs=tuple(vmem(2)),
-        cost_estimate=pl.CostEstimate(flops=0, bytes_accessed=400_000, transcendentals=0),
-    )(positions, coefficients)
-
-
-def exchange(value, axis, groups=None):
-    return lax.all_to_all(value, axis, split_axis=0, concat_axis=0, tiled=True, axis_index_groups=groups)
+    )(cols, *terms)
+
+
+def side_by_side(value):
+    half = value.shape[0] // 2
+    return jnp.concatenate([value[:half], value[half:]], axis=1)
+
+
+def exchange(value, axis):
+    return lax.all_to_all(value, axis, split_axis=0, concat_axis=0, tiled=True)
+
+
+def from_everyone(value, axis):
+    copies = jnp.broadcast_to(value, (lax.axis_size(axis), *value.shape))
+    return exchange(copies, axis).reshape(-1, value.shape[1])
 
 
 def on_device(positions, coefficients, atom_pairs, pair_scale):
-    row_count, col_count = lax.axis_size("row"), lax.axis_size("col")
-    half = positions.shape[0] // 2
-    to_rows, to_cols = pack(positions, coefficients, col_count, row_count // 2)
-    scale = scale_table(atom_pairs, pair_scale)
-    rows = exchange(to_rows, "col").reshape(-1, 2 * CART)
-    same_core = [list(range(core, row_count, 2)) for core in range(2)]
-    one_chip = [[n, n + 1] for n in range(0, row_count, 2)]
-    cols = exchange(to_cols, "row", same_core).reshape(-1, 4 * CART)
-    cols = lax.all_gather(cols, "row", axis=0, tiled=True, axis_index_groups=one_chip)
-    partial = tile_apply(rows, cols, scale)
-    arrived = exchange(partial.reshape(col_count, half, 2 * CART), "col")
+    packed = jnp.concatenate([side_by_side(positions), side_by_side(coefficients)], axis=1)
+    rows = from_everyone(packed[:, : 2 * CART], "row")
+    rows, packed = lax.optimization_barrier((rows, packed))
+    cols = from_everyone(packed, "col")
+    partial = tile_apply(cols, row_terms(rows, atom_pairs, pair_scale))
+    arrived = exchange(partial.reshape(lax.axis_size("row"), -1, 2 * CART), "row")
     total = arrived.sum(axis=0)
     return jnp.concatenate([total[:, :CART], total[:, CART:]], axis=0)
 

time: 59.6 us -> 62.6 us (1.050)
  blocking collectives: 32.7 us -> 10.8 us
  waiting for transfers between devices: 3.33 us -> 15.5 us
  local copies, waits for them, and re-layouts: 1.77 us -> 9.77 us
  starting transfers between devices: 9.98 us -> 17.2 us
  Pallas kernels: 10.6 us -> 8.08 us
    all_to_all x2 -> x1, blocking collectives: 28.7 us -> 10.8 us  [exchange(): return lax.all_to_all(value, axis, split_axis=0, concat_axis=0, tiled=True)]
    all_to_all x1 -> x2, waiting for transfers between devices: 3.33 us -> 15.5 us  [exchange(): return lax.all_to_all(value, axis, split_axis=0, concat_axis=0, tiled=True)]
    all_to_all x1 -> x2, starting transfers between devices: 9.98 us -> 17.2 us  [exchange(): return lax.all_to_all(value, axis, split_axis=0, concat_axis=0, tiled=True)]
    unnamed x4 -> x20, local copies, waits for them, and re-layouts: 1.1 us -> 7.48 us
    all_gather x1 -> x0, blocking collectives: 4 us -> none  [on_device(): lax.all_gather(cols, 'row', axis=0, tiled=True, axis_index_groups=one_chip)]
    pallas_call x3 -> x2, Pallas kernels: 10.6 us -> 8.08 us  [the longest x1 6.41 us: tile_apply(): pl.pallas_call(apply_kernel, out_shape=shape(LANES, 2 * CART), in_specs=v...]
    broadcast_in_dim x0 -> x2, local copies, waits for them, and re-layouts: none -> 1.44 us  [from_everyone(): copies = jnp.broadcast_to(value, (lax.axis_size(axis), *value.shape))]
    slice x0 -> x1, local copies, waits for them, and re-layouts: none -> 0.78 us  [side_by_side(): return jnp.concatenate([value[:half], value[half:]], axis=1)]
  transfers between devices with their start and end apart: 1 -> 2, of which waited for: 1 -> 2; matrix products, arithmetic and copies ran while one was open for 1% -> 0% of each run, Pallas kernels for 4% -> 3%
where the time goes in v2:
time: 62.6 us; the launch traced here: 62.2 us
  starting transfers between devices  17.2 us (27%)
  waiting for transfers between devices  15.5 us (25%)
  blocking collectives  10.8 us (17%)
  local copies, waits for them, and re-layouts  9.77 us (16%)
  Pallas kernels  8.08 us (13%)
  other arithmetic  0.79 us (1%)
    all_to_all x2, starting transfers between devices, exchange(): return lax.all_to_all(value, axis, split_axis=0, concat_axis=0, tiled=True)  17.2 us
    all_to_all x2, waiting for transfers between devices, exchange(): return lax.all_to_all(value, axis, split_axis=0, concat_axis=0, tiled=True)  15.5 us
    all_to_all x1, blocking collectives, exchange(): return lax.all_to_all(value, axis, split_axis=0, concat_axis=0, tiled=True)  10.8 us
    unnamed x20, local copies, waits for them, and re-layouts  7.48 us
    pallas_call x1, Pallas kernels, tile_apply(): pl.pallas_call(apply_kernel, out_shape=shape(LANES, 2 * CART), in_specs=v...  6.41 us
    pallas_call x1, Pallas kernels, row_terms(): pl.pallas_call(rows_kernel, out_shape=(shape(ROWS, LANES), shape(2, 3, WR...  1.68 us
    broadcast_in_dim x2, local copies, waits for them, and re-layouts, from_everyone(): copies = jnp.broadcast_to(value, (lax.axis_size(axis), *value.shape))  1.44 us
  transfers between devices with their start and end apart: 2, of which 2 were waited for; matrix products, arithmetic and copies ran while one was open for 0% of the time, Pallas kernels for 3%

profile of v2, /device:TPU:1, one launch (start us, length us, event | category | flops | bytes accessed | tf_op | source)
XLA Modules:
  0.0 62.2 jit_solution(6020681704420082770)
XLA Ops:
  0.0 0.8 %fusion = (f32[8,147]{1,0:T(8,128)S(1)}, f32[8,147]{1,0:T(8,128)S(1)}, f32[8,147]{1,0:T(8,128)S(1)}, f32[8,147]{1,0:T(8,128)S(1)}) fusion(f32[16,147]{1,0:T(8,128)} %param.5, f32[16,147]{1,0:T(8,128)} %param.4), kind=kLoop, calls=%fused_computation.3 | loop fusion | bytes 37632 | tf_op jit(solution)/shard_map/slice | solution.py:249
  0.8 0.1 pad_maximum_fusion.2
  0.9 0.7 %broadcast_in_dim.6 = f32[16,8,294]{2,1,0:T(8,128)} broadcast(f32[8,294]{1,0:T(8,128)S(1)} %pad_maximum_fusion.2), dimensions={1,2} | broadcast | bytes 159936 | tf_op jit(solution)/shard_map/broadcast_in_dim | solution.py:257
  1.6 7.3 %all-to-all-start = ((f32[16,8,294]{2,1,0:T(8,128)}), f32[16,8,294]{2,1,0:T(8,128)S(1)}, u32[]{:S(2)}, u32[]{:S(2)}) async-start(f32[16,8,294]{2,1,0:T(8,128)} %broadcast_in_dim.6), calls=%async_computation | async-start | bytes 393216 | tf_op jit(solution)/shard_map/all_to_all | solution.py:253
  8.9 0.1 pad_maximum_fusion
  9.0 6.6 %all-to-all-done = f32[16,8,294]{2,1,0:T(8,128)S(1)} async-done(((f32[16,8,294]{2,1,0:T(8,128)}), f32[16,8,294]{2,1,0:T(8,128)S(1)}, u32[]{:S(2)}, u32[]{:S(2)}) %all-to-all-start) | async-done | bytes 150560 | tf_op jit(solution)/shard_map/all_to_all | solution.py:253
  15.6 0.7 %broadcast_in_dim.7 = f32[16,8,588]{2,1,0:T(8,128)} broadcast(f32[8,588]{1,0:T(8,128)S(1)} %pad_maximum_fusion), dimensions={1,2} | broadcast | bytes 319872 | tf_op jit(solution)/shard_map/broadcast_in_dim | solution.py:257
  16.3 9.9 %all-to-all-start.1 = ((f32[16,8,588]{2,1,0:T(8,128)}), f32[16,8,588]{2,1,0:T(8,128)S(1)}, u32[]{:S(2)}, u32[]{:S(2)}) async-start(f32[16,8,588]{2,1,0:T(8,128)} %broadcast_in_dim.7), calls=%async_computation.1 | async-start | bytes 655360 | tf_op jit(solution)/shard_map/all_to_all | solution.py:253
  26.2 0.0 copy-done.9
  26.2 0.0 copy-done
  26.2 1.7 %shard_map.46 = (f32[1344,128]{1,0:T(8,128)S(1)}, f32[2,3,80,128]{3,2,1,0:T(8,128)S(1)}, f32[2,1344,128]{2,1,0:T(8,128)S(1)}, f32[2,1344,128]{2,1,0:T(8,128)S(1)...) custom-call(f32[128,294]{1,0:T(8,128)S(1)} %bitcast.4, ...), custom_call_target="tpu_custom_call" | custom-call | flops 40000000 | bytes 6000000 | tf_op jit(solution)/shard_map/pallas_call | solution.py:203
  27.9 0.8 %copy-done.1 = bf16[256,1344]{1,0:T(8,128)(2,1)} copy-done((bf16[256,1344]{1,0:T(8,128)(2,1)}, bf16[256,1344]{1,0:T(8,128)(2,1)S(1)}, u32[]{:S(2)}) %copy-start.1) | copy-done | bytes 688152
  28.8 0.9 %copy-done.3 = bf16[256,1344]{1,0:T(8,128)(2,1)} copy-done((bf16[256,1344]{1,0:T(8,128)(2,1)}, bf16[256,1344]{1,0:T(8,128)(2,1)S(1)}, u32[]{:S(2)}) %copy-start.3) | copy-done | bytes 688152
  29.6 0.9 %copy-done.5 = f32[1344,128]{1,0:T(8,128)} copy-done((f32[1344,128]{1,0:T(8,128)}, f32[1344,128]{1,0:T(8,128)S(1)}, u32[]{:S(2)}) %copy-start.5) | copy-done | bytes 688152
  30.5 0.7 %copy-done.7 = f32[256,128]{1,0:T(8,128)} copy-done((f32[256,128]{1,0:T(8,128)}, f32[256,128]{1,0:T(8,128)S(1)}, u32[]{:S(2)}) %copy-start.7) | copy-done | bytes 131096
  31.2 8.9 %all-to-all-done.1 = f32[16,8,588]{2,1,0:T(8,128)S(1)} async-done(((f32[16,8,588]{2,1,0:T(8,128)}), f32[16,8,588]{2,1,0:T(8,128)S(1)}, u32[]{:S(2)}, u32[]{:S(2)}) %all-to-all-start.1) | async-done | bytes 301088 | tf_op jit(solution)/shard_map/all_to_all | solution.py:253
  40.0 1.1 %copy-done.2 = bf16[256,1344]{1,0:T(8,128)(2,1)S(1)} copy-done((bf16[256,1344]{1,0:T(8,128)(2,1)S(1)}, bf16[256,1344]{1,0:T(8,128)(2,1)}, u32[]{:S(2)}) %copy-start.2) | copy-done | bytes 688152
  41.1 1.1 %copy-done.4 = bf16[256,1344]{1,0:T(8,128)(2,1)S(1)} copy-done((bf16[256,1344]{1,0:T(8,128)(2,1)S(1)}, bf16[256,1344]{1,0:T(8,128)(2,1)}, u32[]{:S(2)}) %copy-start.4) | copy-done | bytes 688152
  42.3 1.1 %copy-done.6 = f32[1344,128]{1,0:T(8,128)S(1)} copy-done((f32[1344,128]{1,0:T(8,128)S(1)}, f32[1344,128]{1,0:T(8,128)}, u32[]{:S(2)}) %copy-start.6) | copy-done | bytes 688152
  43.4 0.9 %copy-done.8 = f32[256,128]{1,0:T(8,128)S(1)} copy-done((f32[256,128]{1,0:T(8,128)S(1)}, f32[256,128]{1,0:T(8,128)}, u32[]{:S(2)}) %copy-start.8) | copy-done | bytes 131096
  44.3 6.4 %shard_map.47 = f32[128,294]{1,0:T(8,128)S(1)} custom-call(f32[128,588]{1,0:T(8,128)S(1)} %bitcast.3, f32[1344,128]{1,0:T(8,128)S(1)} %copy-done.6, f32[2,3,80,128]{3,2,1,0:T(8,128)S(1)} %get-tuple-element.17.rows_w, f32[2,1344,128]{2,1,0:T(8,128)S(1)} %get-tuple-element.18.row_x, f32[2,1344,128]{2,1,0:T(8,128)S(1)} %get-tuple-element.19.row_weight, ...), custom_call_target="tpu_custom_call" | custom-call | flops 2000000000 | bytes 6000000 | tf_op jit(solution)/shard_map/pallas_call | solution.py:225
  50.7 10.8 %all_to_all.15 = f32[16,8,294]{2,1,0:T(8,128)S(1)} all-to-all(f32[16,8,294]{2,1,0:T(8,128)S(1)} %bitcast.5), channel_id=1, replica_groups=mesh['row'=16,'col'=16] {'row'}, dimensions={0} | all-to-all | bytes 301056 | tf_op jit(solution)/shard_map/all_to_all | solution.py:253
  61.5 0.1 fusion.2
  61.5 0.6 pad_maximum_fusion.1
  (12 shorter events, 0.0 us)
Async XLA Ops:
  0.0 26.2 %copy-start.9 = (f32[1176]{0:T(1024)S(1)}, f32[1176]{0:T(1024)}, u32[]{:S(2)}) copy-start(f32[1176]{0:T(1024)} %param.7) | copy-start | bytes 14116
  0.0 26.2 %copy-start = (s32[2,1176]{1,0:T(2,128)S(1)}, s32[2,1176]{1,0:T(2,128)}, u32[]{:S(2)}) copy-start(s32[2,1176]{1,0:T(2,128)} %pairs_ref.1) | copy-start | bytes 28228
  1.6 14.0 %all-to-all-start = ((f32[16,8,294]{2,1,0:T(8,128)}), f32[16,8,294]{2,1,0:T(8,128)S(1)}, u32[]{:S(2)}, u32[]{:S(2)}) async-start(f32[16,8,294]{2,1,0:T(8,128)} %broadcast_in_dim.6), calls=%async_computation | async-start | bytes 393216 | tf_op jit(solution)/shard_map/all_to_all | solution.py:253
  16.3 23.7 %all-to-all-start.1 = ((f32[16,8,588]{2,1,0:T(8,128)}), f32[16,8,588]{2,1,0:T(8,128)S(1)}, u32[]{:S(2)}, u32[]{:S(2)}) async-start(f32[16,8,588]{2,1,0:T(8,128)} %broadcast_in_dim.7), calls=%async_computation.1 | async-start | bytes 655360 | tf_op jit(solution)/shard_map/all_to_all | solution.py:253
  27.9 0.9 %copy-start.1 = (bf16[256,1344]{1,0:T(8,128)(2,1)}, bf16[256,1344]{1,0:T(8,128)(2,1)S(1)}, u32[]{:S(2)}) copy-start(bf16[256,1344]{1,0:T(8,128)(2,1)S(1)} %get-tuple-element.20.rowx_hi) | copy-start | bytes 2064388
  28.8 0.9 %copy-start.3 = (bf16[256,1344]{1,0:T(8,128)(2,1)}, bf16[256,1344]{1,0:T(8,128)(2,1)S(1)}, u32[]{:S(2)}) copy-start(bf16[256,1344]{1,0:T(8,128)(2,1)S(1)} %get-tuple-element.21.rowx_lo) | copy-start | bytes 2064388
  29.6 0.9 %copy-start.5 = (f32[1344,128]{1,0:T(8,128)}, f32[1344,128]{1,0:T(8,128)S(1)}, u32[]{:S(2)}) copy-start(f32[1344,128]{1,0:T(8,128)S(1)} %get-tuple-element.16.scale_ref) | copy-start | bytes 2064388
  30.5 0.7 %copy-start.7 = (f32[256,128]{1,0:T(8,128)}, f32[256,128]{1,0:T(8,128)S(1)}, u32[]{:S(2)}) copy-start(f32[256,128]{1,0:T(8,128)S(1)} %get-tuple-element.22.row_sq) | copy-start | bytes 393220
  40.0 1.1 %copy-start.2 = (bf16[256,1344]{1,0:T(8,128)(2,1)S(1)}, bf16[256,1344]{1,0:T(8,128)(2,1)}, u32[]{:S(2)}) copy-start(bf16[256,1344]{1,0:T(8,128)(2,1)} %copy-done.1) | copy-start | bytes 2064388
  41.1 1.1 %copy-start.4 = (bf16[256,1344]{1,0:T(8,128)(2,1)S(1)}, bf16[256,1344]{1,0:T(8,128)(2,1)}, u32[]{:S(2)}) copy-start(bf16[256,1344]{1,0:T(8,128)(2,1)} %copy-done.3) | copy-start | bytes 2064388
  42.3 1.1 %copy-start.6 = (f32[1344,128]{1,0:T(8,128)S(1)}, f32[1344,128]{1,0:T(8,128)}, u32[]{:S(2)}) copy-start(f32[1344,128]{1,0:T(8,128)} %copy-done.5) | copy-start | bytes 2064388
  43.4 0.9 %copy-start.8 = (f32[256,128]{1,0:T(8,128)S(1)}, f32[256,128]{1,0:T(8,128)}, u32[]{:S(2)}) copy-start(f32[256,128]{1,0:T(8,128)} %copy-done.7) | copy-start | bytes 393220

commit v3 on v1

--- a/solution.py
+++ b/solution.py
@@ -36,20 +36,7 @@
     return lax.dot_general(a, b, (((1,), (0,)), ((), ())), preferred_element_type=f32)
 
 
-def pack_kernel(p_ref, c_ref, rows_ref, cols_ref):
-    half = p_ref.shape[0] // 2
-    p, c = p_ref[...], c_ref[...]
-    for n in range(rows_ref.shape[0]):
-        rows_ref[n, :, 0:CART] = p[:half]
-        rows_ref[n, :, CART : 2 * CART] = p[half:]
-    for n in range(cols_ref.shape[0]):
-        cols_ref[n, :, 0:CART] = p[:half]
-        cols_ref[n, :, CART : 2 * CART] = p[half:]
-        cols_ref[n, :, 2 * CART : 3 * CART] = c[:half]
-        cols_ref[n, :, 3 * CART : 4 * CART] = c[half:]
-
-
-def scale_kernel(pairs_ref, scale_ref, out_ref):
+def spread_scale(pairs_ref, scale_ref, out_ref):
     low, high = pairs_ref[0:1, :], pairs_ref[1:2, :]
     apart = high - low
     near = apart <= HALF
@@ -96,10 +83,11 @@
 
 
 def apply_kernel(
-    rows_ref, cols_ref, scale_ref, out_ref,
-    flat_rows, flat_cols, rows_w, cols_p, cols_c, pair_hi, pair_lo, row_x, row_weight,
+    rows_ref, cols_ref, pairs_ref, pair_scale_ref, out_ref,
+    scale_ref, flat_rows, flat_cols, rows_w, cols_p, cols_c, pair_hi, pair_lo, row_x, row_weight,
     rowx_hi, rowx_lo, grads, back, flat_out,
 ):
+    spread_scale(pairs_ref, pair_scale_ref, scale_ref)
     flat_cols[...] = cols_ref[...].T
     flat_rows[...] = rows_ref[...].T
     for t in range(2):
@@ -199,13 +187,14 @@
     return [pl.BlockSpec(memory_space=pltpu.VMEM)] * count
 
 
-def tile_apply(rows, cols, scale):
+def tile_apply(rows, cols, atom_pairs, pair_scale):
     return pl.pallas_call(
         apply_kernel,
         out_shape=jax.ShapeDtypeStruct(rows.shape, f32),
-        in_specs=vmem(3),
+        in_specs=vmem(4),
         out_specs=vmem(1)[0],
         scratch_shapes=[
+            pltpu.VMEM((ROWS, LANES), f32),
             pltpu.VMEM((2 * CART, LANES), f32),
             pltpu.VMEM((4 * CART, LANES), f32),
             pltpu.VMEM((2, 3, WRAP, LANES), f32),
@@ -221,51 +210,35 @@
             pltpu.VMEM((3, WRAP, LANES), f32),
             pltpu.VMEM((2 * CART, LANES), f32),
         ],
-        compiler_params=pltpu.CompilerParams(vmem_limit_bytes=40 * 1024 * 1024),
-        cost_estimate=pl.CostEstimate(flops=2_000_000_000, bytes_accessed=2_000_000, transcendentals=1_000_000),
-    )(rows, cols, scale)
-
-
-def scale_table(atom_pairs, pair_scale):
-    return pl.pallas_call(
-        scale_kernel,
-        out_shape=jax.ShapeDtypeStruct((ROWS, LANES), f32),
-        in_specs=vmem(2),
-        out_specs=vmem(1)[0],
-        cost_estimate=pl.CostEstimate(flops=20_000_000, bytes_accessed=700_000, transcendentals=0),
-    )(atom_pairs, pair_scale.reshape(1, -1))
-
-
-def pack(positions, coefficients, row_peers, col_peers):
-    half = positions.shape[0] // 2
-    return pl.pallas_call(
-        pack_kernel,
-        out_shape=(
-            jax.ShapeDtypeStruct((row_peers, half, 2 * CART), f32),
-            jax.ShapeDtypeStruct((col_peers, half, 4 * CART), f32),
+        compiler_params=pltpu.CompilerParams(vmem_limit_bytes=32 * 1024 * 1024),
+        cost_estimate=pl.CostEstimate(
+            flops=2_000_000_000, bytes_accessed=2_000_000, transcendentals=1_000_000
         ),
-        in_specs=vmem(2),
-        out_specs=tuple(vmem(2)),
-        cost_estimate=pl.CostEstimate(flops=0, bytes_accessed=400_000, transcendentals=0),
-    )(positions, coefficients)
-
-
-def exchange(value, axis, groups=None):
-    return lax.all_to_all(value, axis, split_axis=0, concat_axis=0, tiled=True, axis_index_groups=groups)
+    )(rows, cols, atom_pairs, pair_scale.reshape(1, -1))
+
+
+def side_by_side(value):
+    half = value.shape[0] // 2
+    return jnp.concatenate([value[:half], value[half:]], axis=1)
+
+
+def exchange(value, axis):
+    return lax.all_to_all(value, axis, split_axis=0, concat_axis=0, tiled=True)
+
+
+def from_everyone(value, axis):
+    copies = jnp.broadcast_to(value, (lax.axis_size(axis), *value.shape))
+    return exchange(copies, axis).reshape(-1, value.shape[1])
 
 
 def on_device(positions, coefficients, atom_pairs, pair_scale):
-    row_count, col_count = lax.axis_size("row"), lax.axis_size("col")
-    half = positions.shape[0] // 2
-    to_rows, to_cols = pack(positions, coefficients, col_count, row_count // 2)
-    scale = scale_table(atom_pairs, pair_scale)
-    rows = exchange(to_rows, "col").reshape(-1, 2 * CART)
-    same_core = [list(range(core, row_count, 2)) for core in range(2)]
-    one_chip = [[n, n + 1] for n in range(0, row_count, 2)]
-    cols = exchange(to_cols, "row", same_core).reshape(-1, 4 * CART)
-    cols = lax.all_gather(cols, "row", axis=0, tiled=True, axis_index_groups=one_chip)
-    partial = tile_apply(rows, cols, scale)
-    arrived = exchange(partial.reshape(col_count, half, 2 * CART), "col")
+    packed = jnp.concatenate([side_by_side(positions), side_by_side(coefficients)], axis=1)
+    chained = (packed[:, : 2 * CART], packed, atom_pairs, pair_scale)
+    rows, *rest = lax.optimization_barrier(chained)
+    rows, cols, *rest = lax.optimization_barrier((from_everyone(rows, "row"), *rest))
+    chained = lax.optimization_barrier((rows, from_everyone(cols, "col"), *rest))
+    partial = tile_apply(*chained)
+    arrived = exchange(partial.reshape(lax.axis_size("row"), -1, 2 * CART), "row")
     total = arrived.sum(axis=0)
     return jnp.concatenate([total[:, :CART], total[:, CART:]], axis=0)
 

time: 59.6 us -> 58 us (0.973)
  blocking collectives: 32.7 us -> 48.1 us
  starting transfers between devices: 9.98 us -> 0 us
  Pallas kernels: 10.6 us -> 7.13 us
  waiting for transfers between devices: 3.33 us -> 0 us
    all_to_all x2 -> x3, blocking collectives: 28.7 us -> 48.1 us  [exchange(): return lax.all_to_all(value, axis, split_axis=0, concat_axis=0, tiled=True)]
    all_to_all x1 -> x0, starting transfers between devices: 9.98 us -> none  [exchange(): lax.all_to_all(value, axis, split_axis=0, concat_axis=0, tiled=True, axis...]
    all_gather x1 -> x0, blocking collectives: 4 us -> none  [on_device(): lax.all_gather(cols, 'row', axis=0, tiled=True, axis_index_groups=one_chip)]
    pallas_call x2 -> x0, Pallas kernels: 3.7 us -> none  [the longest x1 2.15 us: scale_table(): pl.pallas_call(scale_kernel, out_shape=jax.ShapeDtypeStruct((ROWS, LANES)...]
    all_to_all x1 -> x0, waiting for transfers between devices: 3.33 us -> none  [exchange(): lax.all_to_all(value, axis, split_axis=0, concat_axis=0, tiled=True, axis...]
    slice x0 -> x1, local copies, waits for them, and re-layouts: none -> 0.75 us  [side_by_side(): return jnp.concatenate([value[:half], value[half:]], axis=1)]
  transfers between devices with their start and end apart: 1 -> 0, of which waited for: 1 -> 0; matrix products, arithmetic and copies ran while one was open for 1% -> 0% of each run, Pallas kernels for 4% -> 0%
where the time goes in v3:
time: 58 us; the launch traced here: 57.6 us
  blocking collectives  48.1 us (83%)
  Pallas kernels  7.13 us (12%)
  local copies, waits for them, and re-layouts  1.56 us (3%)
  other arithmetic  0.79 us (1%)
    all_to_all x3, blocking collectives, exchange(): return lax.all_to_all(value, axis, split_axis=0, concat_axis=0, tiled=True)  48.1 us
    pallas_call x1, Pallas kernels, tile_apply(): pl.pallas_call(apply_kernel, out_shape=jax.ShapeDtypeStruct(rows.shape, f...  7.13 us

profile of v3, /device:TPU:1, one launch (start us, length us, event | category | flops | bytes accessed | tf_op | source)
XLA Modules:
  0.0 57.6 jit_solution(18215809954711998070)
XLA Ops:
  0.0 0.7 %fusion = (f32[8,147]{1,0:T(8,128)S(1)}, f32[8,147]{1,0:T(8,128)S(1)}, f32[8,147]{1,0:T(8,128)S(1)}, f32[8,147]{1,0:T(8,128)S(1)}) fusion(f32[16,147]{1,0:T(8,128)} %param.5, f32[16,147]{1,0:T(8,128)} %param.4), kind=kLoop, calls=%fused_computation.3 | loop fusion | bytes 37632 | tf_op jit(solution)/shard_map/slice | solution.py:222
  0.8 0.1 pad_maximum_fusion.2
  0.8 0.1 pad_maximum_fusion
  0.9 13.8 %all_to_all.15 = f32[16,8,294]{2,1,0:T(8,128)S(1)} all-to-all(f32[16,8,294]{2,1,0:T(8,128)S(1)} %broadcast_in_dim.6), channel_id=1, replica_groups=mesh['row'=16,'col'=16] {'row'}, dimensions={0} | all-to-all | bytes 301056 | tf_op jit(solution)/shard_map/all_to_all | solution.py:226
  14.8 0.0 copy-start.1
  14.8 23.5 %all_to_all.16 = f32[16,8,588]{2,1,0:T(8,128)S(1)} all-to-all(f32[16,8,588]{2,1,0:T(8,128)S(1)} %broadcast_in_dim.7), channel_id=1, replica_groups=mesh['row'=16,'col'=16] {'col'}, dimensions={0} | all-to-all | bytes 602112 | tf_op jit(solution)/shard_map/all_to_all | solution.py:226
  38.3 0.0 copy-start
  38.3 0.0 copy-done.1
  38.3 0.7 %copy-done = s32[2,1176]{1,0:T(2,128)S(1)} copy-done((s32[2,1176]{1,0:T(2,128)S(1)}, s32[2,1176]{1,0:T(2,128)}, u32[]{:S(2)}) %copy-start) | copy-done | bytes 9432
  39.0 7.1 %shard_map.46 = f32[128,294]{1,0:T(8,128)S(1)} custom-call(f32[128,294]{1,0:T(8,128)S(1)} %bitcast.4, f32[128,588]{1,0:T(8,128)S(1)} %bitcast.3, s32[2,1176]{1,0:T(2,128)S(1)} %copy-done, f32[1,1176]{1,0:T(1,128)S(1)} %reshape.14.pair_scale_ref), custom_call_target="tpu_custom_call" | custom-call | flops 2000000000 | bytes 2000000 | tf_op jit(solution)/shard_map/pallas_call | solution.py:191
  46.1 10.8 %all_to_all.17 = f32[16,8,294]{2,1,0:T(8,128)S(1)} all-to-all(f32[16,8,294]{2,1,0:T(8,128)S(1)} %bitcast.5), channel_id=1, replica_groups=mesh['row'=16,'col'=16] {'row'}, dimensions={0} | all-to-all | bytes 301056 | tf_op jit(solution)/shard_map/all_to_all | solution.py:226
  56.9 0.1 fusion.2
  57.0 0.6 %pad_maximum_fusion.1 = f32[16,147]{1,0:T(8,128)} fusion(f32[8,147]{1,0:T(8,128)S(1)} %get-tuple-element.34, f32[8,147]{1,0:T(8,128)S(1)} %get-tuple-element.33), kind=kLoop, calls=%fused_computation.1 | loop fusion | flops 2352 | bytes 18816 | tf_op jit(solution)/shard_map/concatenate | solution.py:243
  (4 shorter events, 0.1 us)
Async XLA Ops:
  14.8 23.5 %copy-start.1 = (f32[1176]{0:T(1024)S(1)}, f32[1176]{0:T(1024)}, u32[]{:S(2)}) copy-start(f32[1176]{0:T(1024)} %param.7) | copy-start | bytes 14116
  38.3 0.7 %copy-start = (s32[2,1176]{1,0:T(2,128)S(1)}, s32[2,1176]{1,0:T(2,128)}, u32[]{:S(2)}) copy-start(s32[2,1176]{1,0:T(2,128)} %pairs_ref) | copy-start | bytes 28228

commit v4 on v2

v4 whole, which is shorter than its diff:
```python
import math

import jax
import jax.numpy as jnp
from jax import lax
from jax.experimental import pallas as pl
from jax.experimental.pallas import tpu as pltpu
from jax.sharding import PartitionSpec as P

ATOMS = 49
HALF = 24
BLOCK = 48
LAST = HALF * BLOCK
PAIRS = LAST + HALF
ROWS = PAIRS + 8
KDIM = ROWS
WRAP = 72
CART = 3 * ATOMS
LANES = 128

length_scale = 2.0
decay_rate = math.sqrt(5.0) / length_scale
outer_factor = decay_rate * decay_rate / 3.0
radial_factor = decay_rate * decay_rate
f32 = jnp.float32
bf16 = jnp.bfloat16


def halves(value):
    high = value.astype(bf16)
    return high, (value - high.astype(f32)).astype(bf16)


def dot_nt(a, b):
    return lax.dot_general(a, b, (((1,), (1,)), ((), ())), preferred_element_type=f32)


def dot_nn(a, b):
    return lax.dot_general(a, b, (((1,), (0,)), ((), ())), preferred_element_type=f32)


def spread_scale(pairs_ref, scale_ref, out_ref):
    low, high = pairs_ref[0:1, :], pairs_ref[1:2, :]
    apart = high - low
    near = apart <= HALF
    shift = jnp.where(near, apart, ATOMS - apart) - 1
    start = jnp.where(near, low, high)
    count = low.shape[1]
    atom_ids = lax.broadcasted_iota(jnp.int32, (64, count), 0)
    shift_ids = lax.broadcasted_iota(jnp.int32, (32, count), 0)
    at_atom = jnp.where(atom_ids == start, 1.0, 0.0).astype(bf16)
    scaled = jnp.where(shift_ids == shift, scale_ref[...], 0.0)
    top = scaled.astype(bf16)
    rest = scaled - top.astype(f32)
    middle = rest.astype(bf16)
    bottom = (rest - middle.astype(f32)).astype(bf16)
    table = dot_nt(at_atom, top) + dot_nt(at_atom, middle) + dot_nt(at_atom, bottom)
    for d in range(HALF):
        out_ref[d * BLOCK : (d + 1) * BLOCK, :] = jnp.broadcast_to(
            table[0:BLOCK, d : d + 1], (BLOCK, LANES)
        )
    last = jnp.where(start == ATOMS - 1, scaled, 0.0)
    last = jnp.sum(last[0:HALF], axis=1, keepdims=True)
    out_ref[LAST:PAIRS, :] = jnp.broadcast_to(last, (HALF, LANES))


def wrap_rows(flat_ref, start, wrapped_ref, *at):
    for k in range(3):
        base = start + k * ATOMS
        wrapped_ref[(*at, k, slice(0, ATOMS), slice(None))] = flat_ref[base : base + ATOMS, :]
        wrapped_ref[(*at, k, slice(ATOMS, WRAP), slice(None))] = flat_ref[
            base : base + WRAP - ATOMS, :
        ]


def spans_of(wrapped_ref, at, d):
    if d == 0:
        here, there = slice(ATOMS - 1, ATOMS), slice(0, HALF)
    else:
        here, there = slice(0, BLOCK), slice(d, d + BLOCK)
    return [
        wrapped_ref[(*at, k, here, slice(None))] - wrapped_ref[(*at, k, there, slice(None))]
        for k in range(3)
    ]


def rows_of(d):
    return slice((d - 1) * BLOCK, d * BLOCK) if d else slice(LAST, PAIRS)


CHUNKS = ((0, ROWS),)
PARTS = ((768, ROWS), (0, 384), (384, 768))
separations = (*range(1, HALF + 1), 0)


def fold8(value):
    total = value[0:8]
    for n in range(1, value.shape[0] // 8):
        total = total + value[8 * n : 8 * n + 8]
    return total


def rows_kernel(
    rows_ref, pairs_ref, pair_scale_ref,
    scale_ref, rows_w, rowx_hi, rowx_lo, row_sq,
    flat_rows, row_x,
):
    spread_scale(pairs_ref, pair_scale_ref, scale_ref)
    flat_rows[...] = rows_ref[...].T
    for t in range(2):
        wrap_rows(flat_rows, t * CART, rows_w, t)
    nothing = jnp.zeros((8, LANES), f32)
    for t in range(2):
        for d in separations:
            at = rows_of(d)
            spans = spans_of(rows_w, (t,), d)
            inverse = lax.rsqrt(spans[0] * spans[0] + spans[1] * spans[1] + spans[2] * spans[2])
            x = scale_ref[at, :] * inverse
            row_x[t, at, :] = x
        row_x[t, PAIRS:ROWS, :] = nothing
        sq = 0.0
        for start in range(0, ROWS, LANES):
            stop = min(start + LANES, ROWS)
            turned = row_x[t, start:stop, :].T
            high = turned.astype(bf16)
            rest = turned - high.astype(f32)
            at = slice(t * LANES, (t + 1) * LANES)
            rowx_hi[at, start:stop] = high
            rowx_lo[at, start:stop] = rest.astype(bf16)
            sq = sq + jnp.sum(turned * turned, axis=1, keepdims=True)
        row_sq[t * LANES : (t + 1) * LANES, :] = jnp.broadcast_to(sq, (LANES, LANES))


def apply_kernel(
    cols_ref, scale_ref, rows_w, rowx_hi, rowx_lo, row_sq, out_ref,
    flat_cols, cols_p, cols_c, pair_hi, pair_lo, grads, back, flat_out,
):
    flat_cols[...] = cols_ref[...].T
    for t in range(2):
        wrap_rows(flat_cols, t * CART, cols_p, t)
        wrap_rows(flat_cols, (2 + t) * CART, cols_c, t)

    extra = jnp.where(lax.broadcasted_iota(jnp.int32, (8, LANES), 0) == 0, 1.0, 0.0)
    nothing = jnp.zeros((8, LANES), f32)
    col_sq, col_xu = [], []
    for t in range(2):
        sq, xu = nothing, nothing
        lanes_x = slice(t * LANES, (t + 1) * LANES)
        lanes_u = slice((2 + t) * LANES, (3 + t) * LANES)
        for d in separations:
            spans = spans_of(cols_p, (t,), d)
            moves = spans_of(cols_c, (t,), d)
            inverse = lax.rsqrt(spans[0] * spans[0] + spans[1] * spans[1] + spans[2] * spans[2])
            along = spans[0] * moves[0] + spans[1] * moves[1] + spans[2] * moves[2]
            x = scale_ref[rows_of(d), :] * inverse
            u = -(x * inverse * inverse) * along
            sq = sq + fold8(x * x)
            xu = xu + fold8(x * u)
            at = rows_of(d)
            if d == 0:
                x, u = jnp.concatenate([x, extra], 0), jnp.concatenate([u, nothing], 0)
                at = slice(LAST, ROWS)
            pair_hi[at, lanes_x], pair_lo[at, lanes_x] = halves(x)
            pair_hi[at, lanes_u], pair_lo[at, lanes_u] = halves(u)
        col_sq.append(jnp.sum(sq, axis=0, keepdims=True))
        col_xu.append(jnp.sum(xu, axis=0, keepdims=True))

    count = 2 * LANES
    products, low_low = 0.0, 0.0
    for start, stop in CHUNKS:
        at = slice(start, stop)
        high, low = rowx_hi[:, at], rowx_lo[:, at]
        products = (
            products
            + dot_nn(high, pair_hi[at, :])
            + dot_nn(high, pair_lo[at, :])
            + dot_nn(low, pair_hi[at, :])
        )
        low_low = low_low + dot_nn(low, pair_lo[at, :count])
    gram = products[:, :count] + low_low
    sq_dist = row_sq[:, 0:1] + jnp.concatenate(col_sq, axis=1) - 2.0 * gram
    radius = jnp.sqrt(jnp.maximum(sq_dist, 0.0))
    envelope = outer_factor * jnp.exp(-decay_rate * radius)
    direct = envelope * (1.0 + decay_rate * radius)
    bent = (radial_factor * envelope) * (products[:, count:] - jnp.concatenate(col_xu, axis=1))
    high, low = halves(jnp.concatenate([bent, direct], axis=1))
    for start, stop in PARTS:
        part_hi, part_lo = pair_hi[start:stop, :], pair_lo[start:stop, :]
        grads[start:stop, :] = (
            dot_nt(part_hi, high) + dot_nt(part_lo, high) + dot_nt(part_hi, low)
        )

    for t in range(2):
        lanes = slice(t * LANES, (t + 1) * LANES)
        bend = grads[PAIRS : PAIRS + 1, lanes]

        def terms_of(d):
            at = rows_of(d)
            spans = spans_of(rows_w, (t,), d)
            inverse = lax.rsqrt(spans[0] * spans[0] + spans[1] * spans[1] + spans[2] * spans[2])
            x = scale_ref[at, :] * inverse
            pull = (x * inverse * inverse) * (grads[at, lanes] - bend * x)
            return [pull * span for span in spans]

        back[t] = jnp.zeros(back.shape[1:], f32)
        for k, term in enumerate(terms_of(0)):
            back[t, k, 0:HALF, :] = term
            back[t, k, ATOMS - 1 : ATOMS, :] = -jnp.sum(term, axis=0, keepdims=True)
        here = [jnp.zeros((BLOCK, LANES), f32) for _ in range(3)]
        for shift in range(1, 9):
            there = [None] * 3
            for step in range(3):
                for k, term in enumerate(terms_of(shift + 8 * step)):
                    here[k] = here[k] + term
                    if step == 0:
                        there[k] = [term[8 * n : 8 * n + 8] for n in range(BLOCK // 8)]
                    else:
                        for n in range(BLOCK // 8):
                            piece = term[8 * n : 8 * n + 8]
                            if step + n < len(there[k]):
                                there[k][step + n] = there[k][step + n] + piece
                            else:
                                there[k].append(piece)
            for k in range(3):
                total = jnp.concatenate(there[k], axis=0)
                at = slice(shift, shift + total.shape[0])
                back[t, k, at, :] = back[t, k, at, :] + total
        for k in range(3):
            back[t, k, 0:BLOCK, :] = back[t, k, 0:BLOCK, :] - here[k]
            back[t, k, 0 : WRAP - ATOMS, :] = back[t, k, 0 : WRAP - ATOMS, :] + back[t, k, ATOMS:WRAP, :]
            base = t * CART + k * ATOMS
            flat_out[base : base + ATOMS, :] = back[t, k, 0:ATOMS, :]
    out_ref[...] = flat_out[...].T


def vmem(count):
    return [pl.BlockSpec(memory_space=pltpu.VMEM)] * count


def shape(*dims, kind=f32):
    return jax.ShapeDtypeStruct(dims, kind)


params = pltpu.CompilerParams(vmem_limit_bytes=12 * 1024 * 1024)


def row_terms(rows, atom_pairs, pair_scale):
    return pl.pallas_call(
        rows_kernel,
        out_shape=(
            shape(ROWS, LANES),
            shape(2, 3, WRAP, LANES),
            shape(2 * LANES, KDIM, kind=bf16),
            shape(2 * LANES, KDIM, kind=bf16),
            shape(2 * LANES, LANES),
        ),
        in_specs=vmem(3),
        out_specs=tuple(vmem(5)),
        scratch_shapes=[pltpu.VMEM((2 * CART, LANES), f32), pltpu.VMEM((2, ROWS, LANES), f32)],
        compiler_params=params,
        cost_estimate=pl.CostEstimate(
            flops=40_000_000, bytes_accessed=6_000_000, transcendentals=300_000
        ),
    )(rows, atom_pairs, pair_scale.reshape(1, -1))


def cols_apply(cols, terms):
    return pl.pallas_call(
        apply_kernel,
        out_shape=shape(LANES, 2 * CART),
        in_specs=vmem(1 + len(terms)),
        out_specs=vmem(1)[0],
        scratch_shapes=[
            pltpu.VMEM((4 * CART, LANES), f32),
            pltpu.VMEM((2, 3, WRAP, LANES), f32),
            pltpu.VMEM((2, 3, WRAP, LANES), f32),
            pltpu.VMEM((KDIM, 4 * LANES), bf16),
            pltpu.VMEM((KDIM, 4 * LANES), bf16),
            pltpu.VMEM((ROWS, 2 * LANES), f32),
            pltpu.VMEM((2, 3, WRAP, LANES), f32),
            pltpu.VMEM((2 * CART, LANES), f32),
        ],
        compiler_params=params,
        cost_estimate=pl.CostEstimate(
            flops=2_000_000_000, bytes_accessed=6_000_000, transcendentals=500_000
        ),
    )(cols, *terms)


def tile_apply(rows, cols, atom_pairs, pair_scale):
    return cols_apply(cols, row_terms(rows, atom_pairs, pair_scale))


def side_by_side(value):
    half = value.shape[0] // 2
    return jnp.concatenate([value[:half], value[half:]], axis=1)


def exchange(value, axis):
    return lax.all_to_all(value, axis, split_axis=0, concat_axis=0, tiled=True)


def from_everyone(value, axis):
    copies = jnp.broadcast_to(value, (lax.axis_size(axis), *value.shape))
    return exchange(copies, axis).reshape(-1, value.shape[1])


def on_device(positions, coefficients, atom_pairs, pair_scale):
    packed = jnp.concatenate([side_by_side(positions), side_by_side(coefficients)], axis=1)
    rows, *rest = lax.optimization_barrier((packed[:, : 2 * CART], packed, atom_pairs, pair_scale))
    chained = lax.optimization_barrier((from_everyone(rows, "row"), *rest))
    rows, packed, atom_pairs, pair_scale = chained
    cols = from_everyone(packed, "col")
    partial = tile_apply(rows, cols, atom_pairs, pair_scale)
    arrived = exchange(partial.reshape(lax.axis_size("row"), -1, 2 * CART), "row")
    total = arrived.sum(axis=0)
    return jnp.concatenate([total[:, :CART], total[:, CART:]], axis=0)


def solution(mesh):
    in_specs = (P(("row", "col"), None), P(("row", "col"), None), P(), P())
    out_specs = P(("row", "col"), None)
    return jax.shard_map(
        on_device, mesh=mesh, in_specs=in_specs, out_specs=out_specs, check_vma=False
    )
```

time: 62.6 us -> 56.2 us (0.90)
  blocking collectives: 10.8 us -> 24.6 us
  local copies, waits for them, and re-layouts: 9.77 us -> 2.26 us
  starting transfers between devices: 17.2 us -> 9.98 us
  waiting for transfers between devices: 15.5 us -> 11.7 us
  Pallas kernels: 8.08 us -> 6.41 us
    all_to_all x1 -> x2, blocking collectives: 10.8 us -> 24.6 us  [exchange(): return lax.all_to_all(value, axis, split_axis=0, concat_axis=0, tiled=True)]
    all_to_all x2 -> x1, starting transfers between devices: 17.2 us -> 9.98 us  [exchange(): return lax.all_to_all(value, axis, split_axis=0, concat_axis=0, tiled=True)]
    unnamed x20 -> x4, local copies, waits for them, and re-layouts: 7.48 us -> 0.69 us
    all_to_all x2 -> x1, waiting for transfers between devices: 15.5 us -> 11.7 us  [exchange(): return lax.all_to_all(value, axis, split_axis=0, concat_axis=0, tiled=True)]
    pallas_call x1, Pallas kernels: 6.41 us -> 5.02 us  [cols_apply(): pl.pallas_call(apply_kernel, out_shape=shape(LANES, 2 * CART), in_specs=v...]
    broadcast_in_dim x2, local copies, waits for them, and re-layouts: 1.44 us -> 0.75 us  [from_everyone(): copies = jnp.broadcast_to(value, (lax.axis_size(axis), *value.shape))]
  transfers between devices with their start and end apart: 2 -> 1, of which waited for: 2 -> 1; matrix products, arithmetic and copies ran while one was open for 0% -> 0% of each run, Pallas kernels for 3% -> 2%
where the time goes in v4:
time: 56.2 us; the launch traced here: 55.8 us
  blocking collectives  24.6 us (44%)
  waiting for transfers between devices  11.7 us (21%)
  starting transfers between devices  9.98 us (18%)
  Pallas kernels  6.41 us (11%)
  local copies, waits for them, and re-layouts  2.26 us (4%)
  other arithmetic  0.79 us (1%)
    all_to_all x2, blocking collectives, exchange(): return lax.all_to_all(value, axis, split_axis=0, concat_axis=0, tiled=True)  24.6 us
    all_to_all x1, waiting for transfers between devices, exchange(): return lax.all_to_all(value, axis, split_axis=0, concat_axis=0, tiled=True)  11.7 us
    all_to_all x1, starting transfers between devices, exchange(): return lax.all_to_all(value, axis, split_axis=0, concat_axis=0, tiled=True)  9.98 us
    pallas_call x1, Pallas kernels, cols_apply(): pl.pallas_call(apply_kernel, out_shape=shape(LANES, 2 * CART), in_specs=v...  5.02 us
    pallas_call x1, Pallas kernels, row_terms(): pl.pallas_call(rows_kernel, out_shape=(shape(ROWS, LANES), shape(2, 3, WR...  1.39 us
  transfers between devices with their start and end apart: 1, of which 1 were waited for; matrix products, arithmetic and copies ran while one was open for 0% of the time, Pallas kernels for 2%

profile of v4, /device:TPU:1, one launch (start us, length us, event | category | flops | bytes accessed | tf_op | source)
XLA Modules:
  0.0 55.8 jit_solution(5648571557940258445)
XLA Ops:
  0.0 0.7 %fusion = (f32[8,147]{1,0:T(8,128)S(1)}, f32[8,147]{1,0:T(8,128)S(1)}, f32[8,147]{1,0:T(8,128)S(1)}, f32[8,147]{1,0:T(8,128)S(1)}) fusion(f32[16,147]{1,0:T(8,128)} %param.5, f32[16,147]{1,0:T(8,128)} %param.4), kind=kLoop, calls=%fused_computation.3 | loop fusion | bytes 37632 | tf_op jit(solution)/shard_map/slice | solution.py:296
  0.8 0.1 pad_maximum_fusion.2
  0.8 0.1 pad_maximum_fusion
  0.9 13.8 %all_to_all.15 = f32[16,8,294]{2,1,0:T(8,128)S(1)} all-to-all(f32[16,8,294]{2,1,0:T(8,128)S(1)} %broadcast_in_dim.6), channel_id=1, replica_groups=mesh['row'=16,'col'=16] {'row'}, dimensions={0} | all-to-all | bytes 301056 | tf_op jit(solution)/shard_map/all_to_all | solution.py:300
  14.7 0.7 %broadcast_in_dim.7 = f32[16,8,588]{2,1,0:T(8,128)} broadcast(f32[8,588]{1,0:T(8,128)S(1)} %pad_maximum_fusion), dimensions={1,2} | broadcast | bytes 319872 | tf_op jit(solution)/shard_map/broadcast_in_dim | solution.py:304
  15.5 0.0 copy-start.1
  15.5 10.0 %all-to-all-start.1 = ((f32[16,8,588]{2,1,0:T(8,128)}), f32[16,8,588]{2,1,0:T(8,128)S(1)}, u32[]{:S(2)}, u32[]{:S(2)}) async-start(f32[16,8,588]{2,1,0:T(8,128)} %broadcast_in_dim.7), calls=%async_computation.1 | async-start | bytes 655360 | tf_op jit(solution)/shard_map/all_to_all | solution.py:300
  25.5 0.0 copy-done.1
  25.5 0.0 copy-start
  25.5 0.7 %copy-done = s32[2,1176]{1,0:T(2,128)S(1)} copy-done((s32[2,1176]{1,0:T(2,128)S(1)}, s32[2,1176]{1,0:T(2,128)}, u32[]{:S(2)}) %copy-start) | copy-done | bytes 9432
  26.2 1.4 %shard_map.46 = (f32[1184,128]{1,0:T(8,128)S(1)}, f32[2,3,72,128]{3,2,1,0:T(8,128)S(1)}, bf16[256,1184]{1,0:T(8,128)(2,1)S(1)}, bf16[256,1184]{1,0:T(8,128)(2,1)S(1)}, f32[256,128]{1,0:T(8,128)S(1)}) custom-call(f32[128,294]{1,0:T(8,128)S(1)} %bitcast.4, s32[2,1176]{1,0:T(2,128)S(1)} %copy-done, f32[1,1176]{1,0:T(1,128)S(1)} %reshape.14.pair_scale_ref), custom_call_target="tpu_custom_call" | custom-call | flops 40000000 | bytes 6000000 | tf_op jit(solution)/shard_map/pallas_call | solution.py:248
  27.6 11.7 %all-to-all-done.1 = f32[16,8,588]{2,1,0:T(8,128)S(1)} async-done(((f32[16,8,588]{2,1,0:T(8,128)}), f32[16,8,588]{2,1,0:T(8,128)S(1)}, u32[]{:S(2)}, u32[]{:S(2)}) %all-to-all-start.1) | async-done | bytes 301088 | tf_op jit(solution)/shard_map/all_to_all | solution.py:300
  39.3 5.0 %shard_map.47 = f32[128,294]{1,0:T(8,128)S(1)} custom-call(f32[128,588]{1,0:T(8,128)S(1)} %bitcast.3, f32[1184,128]{1,0:T(8,128)S(1)} %get-tuple-element.26.scale_ref, f32[2,3,72,128]{3,2,1,0:T(8,128)S(1)} %get-tuple-element.27.rows_w, bf16[256,1184]{1,0:T(8,128)(2,1)S(1)} %get-tuple-element.28.rowx_hi, bf16[256,1184]{1,0:T(8,128)(2,1)S(1)} %get-tuple-element.29.rowx_lo, ...), custom_call_target="tpu_custom_call" | custom-call | flops 2000000000 | bytes 6000000 | tf_op jit(solution)/shard_map/pallas_call | solution.py:268
  44.3 10.8 %all_to_all.16 = f32[16,8,294]{2,1,0:T(8,128)S(1)} all-to-all(f32[16,8,294]{2,1,0:T(8,128)S(1)} %bitcast.5), channel_id=1, replica_groups=mesh['row'=16,'col'=16] {'row'}, dimensions={0} | all-to-all | bytes 301056 | tf_op jit(solution)/shard_map/all_to_all | solution.py:300
  55.1 0.1 fusion.2
  55.2 0.6 %pad_maximum_fusion.1 = f32[16,147]{1,0:T(8,128)} fusion(f32[8,147]{1,0:T(8,128)S(1)} %get-tuple-element.36, f32[8,147]{1,0:T(8,128)S(1)} %get-tuple-element.35), kind=kLoop, calls=%fused_computation.1 | loop fusion | flops 2352 | bytes 18816 | tf_op jit(solution)/shard_map/concatenate | solution.py:317
  (3 shorter events, 0.0 us)
Async XLA Ops:
  15.5 10.0 %copy-start.1 = (f32[1176]{0:T(1024)S(1)}, f32[1176]{0:T(1024)}, u32[]{:S(2)}) copy-start(f32[1176]{0:T(1024)} %param.7) | copy-start | bytes 14116
  15.5 23.8 %all-to-all-start.1 = ((f32[16,8,588]{2,1,0:T(8,128)}), f32[16,8,588]{2,1,0:T(8,128)S(1)}, u32[]{:S(2)}, u32[]{:S(2)}) async-start(f32[16,8,588]{2,1,0:T(8,128)} %broadcast_in_dim.7), calls=%async_computation.1 | async-start | bytes 655360 | tf_op jit(solution)/shard_map/all_to_all | solution.py:300
  25.5 0.7 %copy-start = (s32[2,1176]{1,0:T(2,128)S(1)}, s32[2,1176]{1,0:T(2,128)}, u32[]{:S(2)}) copy-start(s32[2,1176]{1,0:T(2,128)} %pairs_ref) | copy-start | bytes 28228

commit v5 on v4

--- a/solution.py
+++ b/solution.py
@@ -1,3 +1,4 @@
+import functools
 import math
 
 import jax
@@ -14,6 +15,7 @@
 PAIRS = LAST + HALF
 ROWS = PAIRS + 8
 KDIM = ROWS
+HALF_ROWS = 8
 WRAP = 72
 CART = 3 * ATOMS
 LANES = 128
@@ -56,7 +58,7 @@
     bottom = (rest - middle.astype(f32)).astype(bf16)
     table = dot_nt(at_atom, top) + dot_nt(at_atom, middle) + dot_nt(at_atom, bottom)
     for d in range(HALF):
-        out_ref[d * BLOCK : (d + 1) * BLOCK, :] = jnp.broadcast_to(
+        out_ref[rows_of(d + 1), :] = jnp.broadcast_to(
             table[0:BLOCK, d : d + 1], (BLOCK, LANES)
         )
     last = jnp.where(start == ATOMS - 1, scaled, 0.0)
@@ -85,11 +87,14 @@
 
 
 def rows_of(d):
-    return slice((d - 1) * BLOCK, d * BLOCK) if d else slice(LAST, PAIRS)
-
-
-CHUNKS = ((0, ROWS),)
-PARTS = ((768, ROWS), (0, 384), (384, 768))
+    if d == 0:
+        return slice(LAST, PAIRS)
+    place = 3 * ((d - 1) % 8) + (d - 1) // 8
+    return slice(place * BLOCK, (place + 1) * BLOCK)
+
+
+GROUP = 3 * BLOCK
+PARTS = ((7, 9), (1, 3), (3, 5), (5, 7))
 separations = (*range(1, HALF + 1), 0)
 
 
@@ -132,8 +137,8 @@
 
 
 def apply_kernel(
-    cols_ref, scale_ref, rows_w, rowx_hi, rowx_lo, row_sq, out_ref,
-    flat_cols, cols_p, cols_c, pair_hi, pair_lo, grads, back, flat_out,
+    place, cols_ref, scale_ref, rows_w, rowx_hi, rowx_lo, row_sq, out_ref,
+    flat_cols, cols_p, cols_c, pair_hi, pair_lo, col_x, col_weight, grads, back, flat_out,
 ):
     flat_cols[...] = cols_ref[...].T
     for t in range(2):
@@ -144,93 +149,116 @@
     nothing = jnp.zeros((8, LANES), f32)
     col_sq, col_xu = [], []
     for t in range(2):
-        sq, xu = nothing, nothing
+        sq = nothing
         lanes_x = slice(t * LANES, (t + 1) * LANES)
+        for d in separations:
+            spans = spans_of(cols_p, (t,), d)
+            inverse = lax.rsqrt(spans[0] * spans[0] + spans[1] * spans[1] + spans[2] * spans[2])
+            at = rows_of(d)
+            x = scale_ref[at, :] * inverse
+            sq = sq + fold8(x * x)
+            col_x[t, at, :] = x
+            col_weight[t, at, :] = x * inverse * inverse
+            if d == 0:
+                x = jnp.concatenate([x, extra], 0)
+                at = slice(LAST, ROWS)
+            pair_hi[at, lanes_x], pair_lo[at, lanes_x] = halves(x)
+        col_sq.append(jnp.sum(sq, axis=0, keepdims=True))
+
+    count = 2 * LANES
+    turned_hi, turned_lo = rowx_hi[...], rowx_lo[...]
+    gram = (
+        dot_nn(turned_hi, pair_hi[:, :count])
+        + dot_nn(turned_hi, pair_lo[:, :count])
+        + dot_nn(turned_lo, pair_hi[:, :count])
+        + dot_nn(turned_lo, pair_lo[:, :count])
+    )
+
+    for t in range(2):
+        xu = nothing
         lanes_u = slice((2 + t) * LANES, (3 + t) * LANES)
         for d in separations:
             spans = spans_of(cols_p, (t,), d)
             moves = spans_of(cols_c, (t,), d)
-            inverse = lax.rsqrt(spans[0] * spans[0] + spans[1] * spans[1] + spans[2] * spans[2])
+            at = rows_of(d)
             along = spans[0] * moves[0] + spans[1] * moves[1] + spans[2] * moves[2]
-            x = scale_ref[rows_of(d), :] * inverse
-            u = -(x * inverse * inverse) * along
-            sq = sq + fold8(x * x)
-            xu = xu + fold8(x * u)
-            at = rows_of(d)
+            u = -col_weight[t, at, :] * along
+            xu = xu + fold8(col_x[t, at, :] * u)
             if d == 0:
-                x, u = jnp.concatenate([x, extra], 0), jnp.concatenate([u, nothing], 0)
+                u = jnp.concatenate([u, nothing], 0)
                 at = slice(LAST, ROWS)
-            pair_hi[at, lanes_x], pair_lo[at, lanes_x] = halves(x)
             pair_hi[at, lanes_u], pair_lo[at, lanes_u] = halves(u)
-        col_sq.append(jnp.sum(sq, axis=0, keepdims=True))
         col_xu.append(jnp.sum(xu, axis=0, keepdims=True))
 
-    count = 2 * LANES
-    products, low_low = 0.0, 0.0
-    for start, stop in CHUNKS:
-        at = slice(start, stop)
-        high, low = rowx_hi[:, at], rowx_lo[:, at]
-        products = (
-            products
-            + dot_nn(high, pair_hi[at, :])
-            + dot_nn(high, pair_lo[at, :])
-            + dot_nn(low, pair_hi[at, :])
-        )
-        low_low = low_low + dot_nn(low, pair_lo[at, :count])
-    gram = products[:, :count] + low_low
+    cross = (
+        dot_nn(turned_hi, pair_hi[:, count:])
+        + dot_nn(turned_hi, pair_lo[:, count:])
+        + dot_nn(turned_lo, pair_hi[:, count:])
+    )
     sq_dist = row_sq[:, 0:1] + jnp.concatenate(col_sq, axis=1) - 2.0 * gram
     radius = jnp.sqrt(jnp.maximum(sq_dist, 0.0))
     envelope = outer_factor * jnp.exp(-decay_rate * radius)
     direct = envelope * (1.0 + decay_rate * radius)
-    bent = (radial_factor * envelope) * (products[:, count:] - jnp.concatenate(col_xu, axis=1))
+    bent = (radial_factor * envelope) * (cross - jnp.concatenate(col_xu, axis=1))
     high, low = halves(jnp.concatenate([bent, direct], axis=1))
-    for start, stop in PARTS:
-        part_hi, part_lo = pair_hi[start:stop, :], pair_lo[start:stop, :]
-        grads[start:stop, :] = (
-            dot_nt(part_hi, high) + dot_nt(part_lo, high) + dot_nt(part_hi, low)
-        )
-
-    for t in range(2):
-        lanes = slice(t * LANES, (t + 1) * LANES)
+    for t in range(2):
+        back[t] = jnp.zeros(back.shape[1:], f32)
+
+    def multiply(first, end):
+        at = slice((first - 1) * GROUP, ROWS if end == 9 else (end - 1) * GROUP)
+        part_hi, part_lo = pair_hi[at, :], pair_lo[at, :]
+        grads[at, :] = dot_nt(part_hi, high) + dot_nt(part_lo, high) + dot_nt(part_hi, low)
+
+    def terms_of(t, d):
+        at, lanes = rows_of(d), slice(t * LANES, (t + 1) * LANES)
+        spans = spans_of(rows_w, (t,), d)
+        inverse = lax.rsqrt(spans[0] * spans[0] + spans[1] * spans[1] + spans[2] * spans[2])
+        x = scale_ref[at, :] * inverse
         bend = grads[PAIRS : PAIRS + 1, lanes]
-
-        def terms_of(d):
-            at = rows_of(d)
-            spans = spans_of(rows_w, (t,), d)
-            inverse = lax.rsqrt(spans[0] * spans[0] + spans[1] * spans[1] + spans[2] * spans[2])
-            x = scale_ref[at, :] * inverse
-            pull = (x * inverse * inverse) * (grads[at, lanes] - bend * x)
-            return [pull * span for span in spans]
-
-        back[t] = jnp.zeros(back.shape[1:], f32)
-        for k, term in enumerate(terms_of(0)):
-            back[t, k, 0:HALF, :] = term
-            back[t, k, ATOMS - 1 : ATOMS, :] = -jnp.sum(term, axis=0, keepdims=True)
+        pull = (x * inverse * inverse) * (grads[at, lanes] - bend * x)
+        return [pull * span for span in spans]
+
+    def pull_back(t, first, end):
         here = [jnp.zeros((BLOCK, LANES), f32) for _ in range(3)]
-        for shift in range(1, 9):
+        if end == 9:
+            for k, term in enumerate(terms_of(t, 0)):
+                back[t, k, 0:HALF, :] = term
+                back[t, k, ATOMS - 1 : ATOMS, :] = -jnp.sum(term, axis=0, keepdims=True)
+        for shift in range(first, end):
             there = [None] * 3
             for step in range(3):
-                for k, term in enumerate(terms_of(shift + 8 * step)):
+                for k, term in enumerate(terms_of(t, shift + 8 * step)):
                     here[k] = here[k] + term
+                    pieces = [term[8 * n : 8 * n + 8] for n in range(BLOCK // 8)]
                     if step == 0:
-                        there[k] = [term[8 * n : 8 * n + 8] for n in range(BLOCK // 8)]
-                    else:
-                        for n in range(BLOCK // 8):
-                            piece = term[8 * n : 8 * n + 8]
-                            if step + n < len(there[k]):
-                                there[k][step + n] = there[k][step + n] + piece
-                            else:
-                                there[k].append(piece)
+                        there[k] = pieces
+                        continue
+                    for n, piece in enumerate(pieces):
+                        if step + n < len(there[k]):
+                            there[k][step + n] = there[k][step + n] + piece
+                        else:
+                            there[k].append(piece)
             for k in range(3):
                 total = jnp.concatenate(there[k], axis=0)
                 at = slice(shift, shift + total.shape[0])
                 back[t, k, at, :] = back[t, k, at, :] + total
         for k in range(3):
             back[t, k, 0:BLOCK, :] = back[t, k, 0:BLOCK, :] - here[k]
+
+    multiply(*PARTS[0])
+    for n, part in enumerate(PARTS):
+        if n + 1 < len(PARTS):
+            multiply(*PARTS[n + 1])
+        for t in range(2):
+            pull_back(t, *part)
+    for t in range(2):
+        for k in range(3):
             back[t, k, 0 : WRAP - ATOMS, :] = back[t, k, 0 : WRAP - ATOMS, :] + back[t, k, ATOMS:WRAP, :]
             base = t * CART + k * ATOMS
             flat_out[base : base + ATOMS, :] = back[t, k, 0:ATOMS, :]
-    out_ref[...] = flat_out[...].T
+    turned = flat_out[...].T
+    for n, (at, size) in enumerate(place(flat_out.shape[1] // HALF_ROWS)):
+        out_ref[pl.ds(at, size), :] = turned[n * size : (n + 1) * size, :]
 
 
 def vmem(count):
@@ -241,7 +269,7 @@
     return jax.ShapeDtypeStruct(dims, kind)
 
 
-params = pltpu.CompilerParams(vmem_limit_bytes=12 * 1024 * 1024)
+params = pltpu.CompilerParams(vmem_limit_bytes=16 * 1024 * 1024)
 
 
 def row_terms(rows, atom_pairs, pair_scale):
@@ -264,9 +292,9 @@
     )(rows, atom_pairs, pair_scale.reshape(1, -1))
 
 
-def cols_apply(cols, terms):
+def cols_apply(cols, terms, place):
     return pl.pallas_call(
-        apply_kernel,
+        functools.partial(apply_kernel, place),
         out_shape=shape(LANES, 2 * CART),
         in_specs=vmem(1 + len(terms)),
         out_specs=vmem(1)[0],
@@ -276,6 +304,8 @@
             pltpu.VMEM((2, 3, WRAP, LANES), f32),
             pltpu.VMEM((KDIM, 4 * LANES), bf16),
             pltpu.VMEM((KDIM, 4 * LANES), bf16),
+            pltpu.VMEM((2, ROWS, LANES), f32),
+            pltpu.VMEM((2, ROWS, LANES), f32),
             pltpu.VMEM((ROWS, 2 * LANES), f32),
             pltpu.VMEM((2, 3, WRAP, LANES), f32),
             pltpu.VMEM((2 * CART, LANES), f32),
@@ -287,8 +317,12 @@
     )(cols, *terms)
 
 
-def tile_apply(rows, cols, atom_pairs, pair_scale):
-    return cols_apply(cols, row_terms(rows, atom_pairs, pair_scale))
+def as_they_are(count):
+    return [(0, count * HALF_ROWS)]
+
+
+def tile_apply(rows, cols, atom_pairs, pair_scale, place=as_they_are):
+    return cols_apply(cols, row_terms(rows, atom_pairs, pair_scale), place)
 
 
 def side_by_side(value):
@@ -305,13 +339,32 @@
     return exchange(copies, axis).reshape(-1, value.shape[1])
 
 
+def in_groups(value, axis, size):
+    groups = [list(range(n, n + size)) for n in range(0, lax.axis_size(axis), size)]
+    return lax.all_gather(value, axis, axis=0, tiled=True, axis_index_groups=groups)
+
+
+def with_partners(value, axis, steps):
+    count = lax.axis_size(axis)
+    moved = [lax.ppermute(value, axis, [(n, n ^ step) for n in range(count)]) for step in steps]
+    return jnp.concatenate([value, *moved], axis=0)
+
+
+def row_gather(value, axis):
+    return with_partners(in_groups(value, axis, 4), axis, (4, 8, 12))
+
+
+def owners_place(count):
+    own = 4 * (lax.axis_index("row") // 4)
+    size = 4 * HALF_ROWS
+    return [(pl.multiple_of((own ^ step) * HALF_ROWS, size), size) for step in range(0, count, 4)]
+
+
 def on_device(positions, coefficients, atom_pairs, pair_scale):
     packed = jnp.concatenate([side_by_side(positions), side_by_side(coefficients)], axis=1)
-    rows, *rest = lax.optimization_barrier((packed[:, : 2 * CART], packed, atom_pairs, pair_scale))
-    chained = lax.optimization_barrier((from_everyone(rows, "row"), *rest))
-    rows, packed, atom_pairs, pair_scale = chained
     cols = from_everyone(packed, "col")
-    partial = tile_apply(rows, cols, atom_pairs, pair_scale)
+    rows = row_gather(packed[:, : 2 * CART], "row")
+    partial = tile_apply(rows, cols, atom_pairs, pair_scale, owners_place)
     arrived = exchange(partial.reshape(lax.axis_size("row"), -1, 2 * CART), "row")
     total = arrived.sum(axis=0)
     return jnp.concatenate([total[:, :CART], total[:, CART:]], axis=0)

time: 56.2 us -> 49 us (0.87)
  waiting for transfers between devices: 11.7 us -> 3.77 us
  starting transfers between devices: 9.98 us -> 15 us
  blocking collectives: 24.6 us -> 21 us
  local copies, waits for them, and re-layouts: 2.26 us -> 1.59 us
    all_to_all x2 -> x1, blocking collectives: 24.6 us -> 11.4 us  [exchange(): return lax.all_to_all(value, axis, split_axis=0, concat_axis=0, tiled=True)]
    all_to_all x1, waiting for transfers between devices: 11.7 us -> 0.01 us  [exchange(): return lax.all_to_all(value, axis, split_axis=0, concat_axis=0, tiled=True)]
    all_gather x0 -> x1, blocking collectives: none -> 9.6 us  [in_groups(): lax.all_gather(value, axis, axis=0, tiled=True, axis_index_groups=groups)]
    ppermute x0 -> x3, waiting for transfers between devices: none -> 3.77 us  [with_partners(): lax.ppermute(value, axis, [(n, n ^ step) for n in range(count)])]
    ppermute x0 -> x3, starting transfers between devices: none -> 3.4 us  [with_partners(): lax.ppermute(value, axis, [(n, n ^ step) for n in range(count)])]
    all_to_all x1, starting transfers between devices: 9.98 us -> 11.6 us  [exchange(): return lax.all_to_all(value, axis, split_axis=0, concat_axis=0, tiled=True)]
    unnamed x4, local copies, waits for them, and re-layouts: 0.69 us -> 0.01 us
  transfers between devices with their start and end apart: 1 -> 4, of which waited for: 1 -> 2; matrix products, arithmetic and copies ran while one was open for 0% -> 0% of each run, Pallas kernels for 2% -> 3%
where the time goes in v5:
time: 49 us; the launch traced here: 48.6 us
  blocking collectives  21 us (43%)
  starting transfers between devices  15 us (31%)
  Pallas kernels  6.35 us (13%)
  waiting for transfers between devices  3.77 us (8%)
  local copies, waits for them, and re-layouts  1.59 us (3%)
  other arithmetic  0.8 us (2%)
    all_to_all x1, starting transfers between devices, exchange(): return lax.all_to_all(value, axis, split_axis=0, concat_axis=0, tiled=True)  11.6 us
    all_to_all x1, blocking collectives, exchange(): return lax.all_to_all(value, axis, split_axis=0, concat_axis=0, tiled=True)  11.4 us
    all_gather x1, blocking collectives, in_groups(): lax.all_gather(value, axis, axis=0, tiled=True, axis_index_groups=groups)  9.6 us
    pallas_call x1, Pallas kernels, cols_apply(): pl.pallas_call(functools.partial(apply_kernel, place), out_shape=shape(LA...  4.97 us
    ppermute x3, waiting for transfers between devices, with_partners(): lax.ppermute(value, axis, [(n, n ^ step) for n in range(count)])  3.77 us
    ppermute x3, starting transfers between devices, with_partners(): lax.ppermute(value, axis, [(n, n ^ step) for n in range(count)])  3.4 us
    pallas_call x1, Pallas kernels, row_terms(): pl.pallas_call(rows_kernel, out_shape=(shape(ROWS, LANES), shape(2, 3, WR...  1.39 us
  transfers between devices with their start and end apart: 4, of which 2 were waited for; matrix products, arithmetic and copies ran while one was open for 0% of the time, Pallas kernels for 3%

profile of v5, /device:TPU:1, one launch (start us, length us, event | category | flops | bytes accessed | tf_op | source)
XLA Modules:
  0.0 48.6 jit_solution(11533320288932012208)
XLA Ops:
  0.0 0.7 %fusion = (f32[8,147]{1,0:T(8,128)S(1)}, f32[8,147]{1,0:T(8,128)S(1)}, f32[8,147]{1,0:T(8,128)S(1)}, f32[8,147]{1,0:T(8,128)S(1)}) fusion(f32[16,147]{1,0:T(8,128)} %param.4, f32[16,147]{1,0:T(8,128)} %param.5), kind=kLoop, calls=%fused_computation.4 | loop fusion | bytes 37632 | tf_op jit(solution)/shard_map/slice | solution.py:330
  0.8 0.1 pad_maximum_fusion.1
  0.8 0.8 %broadcast_in_dim.3 = f32[16,8,588]{2,1,0:T(8,128)} broadcast(f32[8,588]{1,0:T(8,128)S(1)} %pad_maximum_fusion.1), dimensions={1,2} | broadcast | bytes 319872 | tf_op jit(solution)/shard_map/broadcast_in_dim | solution.py:338
  1.6 11.6 %all-to-all-start = ((f32[16,8,588]{2,1,0:T(8,128)}), f32[16,8,588]{2,1,0:T(8,128)S(1)}, u32[]{:S(2)}, u32[]{:S(2)}) async-start(f32[16,8,588]{2,1,0:T(8,128)} %broadcast_in_dim.3), calls=%async_computation | async-start | bytes 655360 | tf_op jit(solution)/shard_map/all_to_all | solution.py:334
  13.2 0.1 pad_maximum_fusion.3
  13.2 0.0 copy-start.1
  13.2 9.6 %all_gather.3 = f32[32,294]{1,0:T(8,128)S(1)} all-gather(f32[8,294]{1,0:T(8,128)S(1)} %pad_maximum_fusion.3), channel_id=1, replica_groups={{0,16,32,48},{64,80,96,112},{128,144,160,176},{192,208,224,240},{1,17,3..., dimensions={0}, use_global_device_ids=true | all-gather | bytes 47040 | tf_op jit(solution)/shard_map/all_gather | solution.py:344
  22.9 2.7 %collective-permute-start.2 = (f32[32,294]{1,0:T(8,128)S(1)}, f32[32,294]{1,0:T(8,128)S(1)}, u32[]{:S(2)}, u32[]{:S(2)}) collective-permute-start(f32[32,294]{1,0:T(8,128)S(1)} %all_gather.3), channel_id=1, source_target_pairs={{0,192},{16,208},{32,224},{48,240},{64,128},{80,144},{96,160},{112... | collective-permute-start | bytes 112904 | tf_op jit(solution)/shard_map/ppermute | solution.py:349
  25.6 0.3 collective-permute-start.1
  25.9 0.3 collective-permute-start
  26.3 0.0 copy-done.1
  26.3 0.0 copy-start
  26.3 1.1 %collective-permute-done.2 = f32[32,294]{1,0:T(8,128)S(1)} collective-permute-done((f32[32,294]{1,0:T(8,128)S(1)}, f32[32,294]{1,0:T(8,128)S(1)}, u32[]{:S(2)}, u32[]{:S(2)}) %collective-permute-start.2) | collective-permute-done | bytes 37664 | tf_op jit(solution)/shard_map/ppermute | solution.py:349
  27.4 2.7 %collective-permute-done.1 = f32[32,294]{1,0:T(8,128)S(1)} collective-permute-done((f32[32,294]{1,0:T(8,128)S(1)}, f32[32,294]{1,0:T(8,128)S(1)}, u32[]{:S(2)}, u32[]{:S(2)}) %collective-permute-start.1) | collective-permute-done | bytes 37664 | tf_op jit(solution)/shard_map/ppermute | solution.py:349
  30.0 0.0 collective-permute-done
  30.1 0.0 copy-done
  30.1 1.4 %shard_map.46 = (f32[1184,128]{1,0:T(8,128)S(1)}, f32[2,3,72,128]{3,2,1,0:T(8,128)S(1)}, bf16[256,1184]{1,0:T(8,128)(2,1)S(1)}, bf16[256,1184]{1,0:T(8,128)(2,1)S(1)}, f32[256,128]{1,0:T(8,128)S(1)}) custom-call(f32[128,294]{1,0:T(8,128)S(1)} %pad_maximum_fusion.rows_ref, s32[2,1176]{1,0:T(2,128)S(1)} %copy-done, f32[1,1176]{1,0:T(1,128)S(1)} %reshape.10.pair_scale_ref), custom_call_target="tpu_custom_call" | custom-call | flops 40000000 | bytes 6000000 | tf_op jit(solution)/shard_map/pallas_call | solution.py:276
  31.5 0.0 all-to-all-done
  31.5 5.0 %shard_map.47 = f32[128,294]{1,0:T(8,128)S(1)} custom-call(f32[128,588]{1,0:T(8,128)S(1)} %bitcast.2, f32[1184,128]{1,0:T(8,128)S(1)} %get-tuple-element.10.scale_ref, f32[2,3,72,128]{3,2,1,0:T(8,128)S(1)} %get-tuple-element.11.rows_w, bf16[256,1184]{1,0:T(8,128)(2,1)S(1)} %get-tuple-element.12.rowx_hi, bf16[256,1184]{1,0:T(8,128)(2,1)S(1)} %get-tuple-element.13.rowx_lo, ...), custom_call_target="tpu_custom_call" | custom-call | flops 2000000000 | bytes 6000000 | tf_op jit(solution)/shard_map/pallas_call | solution.py:296
  36.4 11.4 %all_to_all.10 = f32[16,8,294]{2,1,0:T(8,128)S(1)} all-to-all(f32[16,8,294]{2,1,0:T(8,128)S(1)} %bitcast.3), channel_id=1, replica_groups=mesh['row'=16,'col'=16] {'row'}, dimensions={0} | all-to-all | bytes 301056 | tf_op jit(solution)/shard_map/all_to_all | solution.py:334
  47.9 0.1 fusion.2
  47.9 0.6 %pad_maximum_fusion.2 = f32[16,147]{1,0:T(8,128)} fusion(f32[8,147]{1,0:T(8,128)S(1)} %get-tuple-element.20, f32[8,147]{1,0:T(8,128)S(1)} %get-tuple-element.19), kind=kLoop, calls=%fused_computation.2 | loop fusion | flops 2352 | bytes 18816 | tf_op jit(solution)/shard_map/concatenate | solution.py:370
  (3 shorter events, 0.0 us)
Async XLA Ops:
  1.6 29.9 %all-to-all-start = ((f32[16,8,588]{2,1,0:T(8,128)}), f32[16,8,588]{2,1,0:T(8,128)S(1)}, u32[]{:S(2)}, u32[]{:S(2)}) async-start(f32[16,8,588]{2,1,0:T(8,128)} %broadcast_in_dim.3), calls=%async_computation | async-start | bytes 655360 | tf_op jit(solution)/shard_map/all_to_all | solution.py:334
  13.2 13.0 %copy-start.1 = (f32[1176]{0:T(1024)S(1)}, f32[1176]{0:T(1024)}, u32[]{:S(2)}) copy-start(f32[1176]{0:T(1024)} %param.7) | copy-start | bytes 14116
  22.9 4.5 %collective-permute-start.2 = (f32[32,294]{1,0:T(8,128)S(1)}, f32[32,294]{1,0:T(8,128)S(1)}, u32[]{:S(2)}, u32[]{:S(2)}) collective-permute-start(f32[32,294]{1,0:T(8,128)S(1)} %all_gather.3), channel_id=1, source_target_pairs={{0,192},{16,208},{32,224},{48,240},{64,128},{80,144},{96,160},{112... | collective-permute-start | bytes 112904 | tf_op jit(solution)/shard_map/ppermute | solution.py:349
  25.6 4.4 %collective-permute-start.1 = (f32[32,294]{1,0:T(8,128)S(1)}, f32[32,294]{1,0:T(8,128)S(1)}, u32[]{:S(2)}, u32[]{:S(2)}) collective-permute-start(f32[32,294]{1,0:T(8,128)S(1)} %all_gather.3), channel_id=1, source_target_pairs={{0,128},{16,144},{32,160},{48,176},{64,192},{80,208},{96,224},{112... | collective-permute-start | bytes 112904 | tf_op jit(solution)/shard_map/ppermute | solution.py:349
  25.9 4.1 %collective-permute-start = (f32[32,294]{1,0:T(8,128)S(1)}, f32[32,294]{1,0:T(8,128)S(1)}, u32[]{:S(2)}, u32[]{:S(2)}) collective-permute-start(f32[32,294]{1,0:T(8,128)S(1)} %all_gather.3), channel_id=1, source_target_pairs={{0,64},{16,80},{32,96},{48,112},{64,0},{80,16},{96,32},{112,48},{1... | collective-permute-start | bytes 112904 | tf_op jit(solution)/shard_map/ppermute | solution.py:349
  26.3 3.8 %copy-start = (s32[2,1176]{1,0:T(2,128)S(1)}, s32[2,1176]{1,0:T(2,128)}, u32[]{:S(2)}) copy-start(s32[2,1176]{1,0:T(2,128)} %pairs_ref.1) | copy-start | bytes 28228

commit v6 on v5

--- a/solution.py
+++ b/solution.py
@@ -351,13 +351,14 @@
 
 
 def row_gather(value, axis):
-    return with_partners(in_groups(value, axis, 4), axis, (4, 8, 12))
+    return in_groups(with_partners(value, axis, (4, 8, 12)), axis, 4)
 
 
 def owners_place(count):
-    own = 4 * (lax.axis_index("row") // 4)
-    size = 4 * HALF_ROWS
-    return [(pl.multiple_of((own ^ step) * HALF_ROWS, size), size) for step in range(0, count, 4)]
+    own = lax.axis_index("row")
+    first = 4 * (own // 4)
+    numbers = [(first ^ step) + n for n in range(4) for step in (0, 4, 8, 12)]
+    return [(pl.multiple_of(at * HALF_ROWS, HALF_ROWS), HALF_ROWS) for at in numbers]
 
 
 def on_device(positions, coefficients, atom_pairs, pair_scale):

time: 49 us -> 46.1 us (0.941)
  blocking collectives: 21 us -> 18.5 us
    all_gather x1, blocking collectives: 9.6 us -> 7.94 us  [in_groups(): lax.all_gather(value, axis, axis=0, tiled=True, axis_index_groups=groups)]
    all_to_all x1, blocking collectives: 11.4 us -> 10.6 us  [exchange(): return lax.all_to_all(value, axis, split_axis=0, concat_axis=0, tiled=True)]
where the time goes in v6:
time: 46.1 us; the launch traced here: 45.8 us
  blocking collectives  18.5 us (40%)
  starting transfers between devices  15 us (33%)
  Pallas kernels  6.36 us (14%)
  waiting for transfers between devices  3.37 us (7%)
  local copies, waits for them, and re-layouts  1.59 us (3%)
  other arithmetic  0.86 us (2%)
    all_to_all x1, starting transfers between devices, exchange(): return lax.all_to_all(value, axis, split_axis=0, concat_axis=0, tiled=True)  11.6 us
    all_to_all x1, blocking collectives, exchange(): return lax.all_to_all(value, axis, split_axis=0, concat_axis=0, tiled=True)  10.6 us
    all_gather x1, blocking collectives, in_groups(): lax.all_gather(value, axis, axis=0, tiled=True, axis_index_groups=groups)  7.94 us
    pallas_call x1, Pallas kernels, cols_apply(): pl.pallas_call(functools.partial(apply_kernel, place), out_shape=shape(LA...  4.97 us
    ppermute x3, starting transfers between devices, with_partners(): lax.ppermute(value, axis, [(n, n ^ step) for n in range(count)])  3.44 us
    ppermute x3, waiting for transfers between devices, with_partners(): lax.ppermute(value, axis, [(n, n ^ step) for n in range(count)])  3.37 us
    pallas_call x1, Pallas kernels, row_terms(): pl.pallas_call(rows_kernel, out_shape=(shape(ROWS, LANES), shape(2, 3, WR...  1.39 us
  transfers between devices with their start and end apart: 4, of which 2 were waited for; matrix products, arithmetic and copies ran while one was open for 0% of the time, Pallas kernels for 3%

profile of v6, /device:TPU:1, one launch (start us, length us, event | category | flops | bytes accessed | tf_op | source)
XLA Modules:
  0.0 45.8 jit_solution(15766384612280616331)
XLA Ops:
  0.0 0.7 %fusion = (f32[8,147]{1,0:T(8,128)S(1)}, f32[8,147]{1,0:T(8,128)S(1)}, f32[8,147]{1,0:T(8,128)S(1)}, f32[8,147]{1,0:T(8,128)S(1)}) fusion(f32[16,147]{1,0:T(8,128)} %param.4, f32[16,147]{1,0:T(8,128)} %param.5), kind=kLoop, calls=%fused_computation.4 | loop fusion | bytes 37632 | tf_op jit(solution)/shard_map/slice | solution.py:330
  0.8 0.1 pad_maximum_fusion.1
  0.8 0.8 %broadcast_in_dim.3 = f32[16,8,588]{2,1,0:T(8,128)} broadcast(f32[8,588]{1,0:T(8,128)S(1)} %pad_maximum_fusion.1), dimensions={1,2} | broadcast | bytes 319872 | tf_op jit(solution)/shard_map/broadcast_in_dim | solution.py:338
  1.6 11.6 %all-to-all-start = ((f32[16,8,588]{2,1,0:T(8,128)}), f32[16,8,588]{2,1,0:T(8,128)S(1)}, u32[]{:S(2)}, u32[]{:S(2)}) async-start(f32[16,8,588]{2,1,0:T(8,128)} %broadcast_in_dim.3), calls=%async_computation | async-start | bytes 655360 | tf_op jit(solution)/shard_map/all_to_all | solution.py:334
  13.2 0.0 copy-start.1
  13.2 0.1 pad_maximum_fusion.3
  13.3 2.8 %collective-permute-start.2 = (f32[8,294]{1,0:T(8,128)S(1)}, f32[8,294]{1,0:T(8,128)S(1)}, u32[]{:S(2)}, u32[]{:S(2)}) collective-permute-start(f32[8,294]{1,0:T(8,128)S(1)} %pad_maximum_fusion.3), channel_id=1, source_target_pairs={{0,192},{16,208},{32,224},{48,240},{64,128},{80,144},{96,160},{112... | collective-permute-start | bytes 28232 | tf_op jit(solution)/shard_map/ppermute | solution.py:349
  16.0 0.3 collective-permute-start.1
  16.4 0.3 collective-permute-start
  16.7 0.0 copy-done.1
  16.7 0.4 collective-permute-done.2
  17.1 3.0 %collective-permute-done.1 = f32[8,294]{1,0:T(8,128)S(1)} collective-permute-done((f32[8,294]{1,0:T(8,128)S(1)}, f32[8,294]{1,0:T(8,128)S(1)}, u32[]{:S(2)}, u32[]{:S(2)}) %collective-permute-start.1) | collective-permute-done | bytes 9440 | tf_op jit(solution)/shard_map/ppermute | solution.py:349
  20.1 0.0 collective-permute-done
  20.1 0.1 pad_maximum_fusion
  20.1 0.0 copy-start
  20.1 7.9 %all_gather.3.rows_ref = f32[128,294]{1,0:T(8,128)S(1)} all-gather(f32[32,294]{1,0:T(8,128)S(1)} %pad_maximum_fusion), channel_id=1, replica_groups={{0,16,32,48},{64,80,96,112},{128,144,160,176},{192,208,224,240},{1,17,3..., dimensions={0}, use_global_device_ids=true | all-gather | bytes 188160 | tf_op jit(solution)/shard_map/all_gather | solution.py:344
  28.1 0.0 copy-done
  28.1 1.4 %shard_map.46 = (f32[1184,128]{1,0:T(8,128)S(1)}, f32[2,3,72,128]{3,2,1,0:T(8,128)S(1)}, bf16[256,1184]{1,0:T(8,128)(2,1)S(1)}, bf16[256,1184]{1,0:T(8,128)(2,1)S(1)}, f32[256,128]{1,0:T(8,128)S(1)}) custom-call(f32[128,294]{1,0:T(8,128)S(1)} %all_gather.3.rows_ref, s32[2,1176]{1,0:T(2,128)S(1)} %copy-done, f32[1,1176]{1,0:T(1,128)S(1)} %reshape.10.pair_scale_ref), custom_call_target="tpu_custom_call" | custom-call | flops 40000000 | bytes 6000000 | tf_op jit(solution)/shard_map/pallas_call | solution.py:276
  29.5 0.0 all-to-all-done
  29.5 5.0 %shard_map.47 = f32[128,294]{1,0:T(8,128)S(1)} custom-call(f32[128,588]{1,0:T(8,128)S(1)} %bitcast.2, f32[1184,128]{1,0:T(8,128)S(1)} %get-tuple-element.10.scale_ref, f32[2,3,72,128]{3,2,1,0:T(8,128)S(1)} %get-tuple-element.11.rows_w, bf16[256,1184]{1,0:T(8,128)(2,1)S(1)} %get-tuple-element.12.rowx_hi, bf16[256,1184]{1,0:T(8,128)(2,1)S(1)} %get-tuple-element.13.rowx_lo, ...), custom_call_target="tpu_custom_call" | custom-call | flops 2000000000 | bytes 6000000 | tf_op jit(solution)/shard_map/pallas_call | solution.py:296
  34.5 10.6 %all_to_all.10 = f32[16,8,294]{2,1,0:T(8,128)S(1)} all-to-all(f32[16,8,294]{2,1,0:T(8,128)S(1)} %bitcast.3), channel_id=1, replica_groups=mesh['row'=16,'col'=16] {'row'}, dimensions={0} | all-to-all | bytes 301056 | tf_op jit(solution)/shard_map/all_to_all | solution.py:334
  45.1 0.1 fusion.2
  45.2 0.6 %pad_maximum_fusion.2 = f32[16,147]{1,0:T(8,128)} fusion(f32[8,147]{1,0:T(8,128)S(1)} %get-tuple-element.20, f32[8,147]{1,0:T(8,128)S(1)} %get-tuple-element.19), kind=kLoop, calls=%fused_computation.2 | loop fusion | flops 2352 | bytes 18816 | tf_op jit(solution)/shard_map/concatenate | solution.py:371
  (2 shorter events, 0.0 us)
Async XLA Ops:
  1.6 27.9 %all-to-all-start = ((f32[16,8,588]{2,1,0:T(8,128)}), f32[16,8,588]{2,1,0:T(8,128)S(1)}, u32[]{:S(2)}, u32[]{:S(2)}) async-start(f32[16,8,588]{2,1,0:T(8,128)} %broadcast_in_dim.3), calls=%async_computation | async-start | bytes 655360 | tf_op jit(solution)/shard_map/all_to_all | solution.py:334
  13.2 3.5 %copy-start.1 = (f32[1176]{0:T(1024)S(1)}, f32[1176]{0:T(1024)}, u32[]{:S(2)}) copy-start(f32[1176]{0:T(1024)} %param.7) | copy-start | bytes 14116
  13.3 3.8 %collective-permute-start.2 = (f32[8,294]{1,0:T(8,128)S(1)}, f32[8,294]{1,0:T(8,128)S(1)}, u32[]{:S(2)}, u32[]{:S(2)}) collective-permute-start(f32[8,294]{1,0:T(8,128)S(1)} %pad_maximum_fusion.3), channel_id=1, source_target_pairs={{0,192},{16,208},{32,224},{48,240},{64,128},{80,144},{96,160},{112... | collective-permute-start | bytes 28232 | tf_op jit(solution)/shard_map/ppermute | solution.py:349
  16.0 4.0 %collective-permute-start.1 = (f32[8,294]{1,0:T(8,128)S(1)}, f32[8,294]{1,0:T(8,128)S(1)}, u32[]{:S(2)}, u32[]{:S(2)}) collective-permute-start(f32[8,294]{1,0:T(8,128)S(1)} %pad_maximum_fusion.3), channel_id=1, source_target_pairs={{0,128},{16,144},{32,160},{48,176},{64,192},{80,208},{96,224},{112... | collective-permute-start | bytes 28232 | tf_op jit(solution)/shard_map/ppermute | solution.py:349
  16.4 3.7 %collective-permute-start = (f32[8,294]{1,0:T(8,128)S(1)}, f32[8,294]{1,0:T(8,128)S(1)}, u32[]{:S(2)}, u32[]{:S(2)}) collective-permute-start(f32[8,294]{1,0:T(8,128)S(1)} %pad_maximum_fusion.3), channel_id=1, source_target_pairs={{0,64},{16,80},{32,96},{48,112},{64,0},{80,16},{96,32},{112,48},{1... | collective-permute-start | bytes 28232 | tf_op jit(solution)/shard_map/ppermute | solution.py:349
  20.1 7.9 %copy-start = (s32[2,1176]{1,0:T(2,128)S(1)}, s32[2,1176]{1,0:T(2,128)}, u32[]{:S(2)}) copy-start(s32[2,1176]{1,0:T(2,128)} %pairs_ref.1) | copy-start | bytes 28228

commit v7 on v6

--- a/solution.py
+++ b/solution.py
@@ -166,13 +166,9 @@
         col_sq.append(jnp.sum(sq, axis=0, keepdims=True))
 
     count = 2 * LANES
-    turned_hi, turned_lo = rowx_hi[...], rowx_lo[...]
-    gram = (
-        dot_nn(turned_hi, pair_hi[:, :count])
-        + dot_nn(turned_hi, pair_lo[:, :count])
-        + dot_nn(turned_lo, pair_hi[:, :count])
-        + dot_nn(turned_lo, pair_lo[:, :count])
-    )
+    turned = jnp.concatenate([rowx_hi[...], rowx_lo[...]], axis=0)
+    with_high, with_low = dot_nn(turned, pair_hi[:, :count]), dot_nn(turned, pair_lo[:, :count])
+    gram = (with_high[:count] + with_high[count:]) + (with_low[:count] + with_low[count:])
 
     for t in range(2):
         xu = nothing
@@ -190,11 +186,8 @@
             pair_hi[at, lanes_u], pair_lo[at, lanes_u] = halves(u)
         col_xu.append(jnp.sum(xu, axis=0, keepdims=True))
 
-    cross = (
-        dot_nn(turned_hi, pair_hi[:, count:])
-        + dot_nn(turned_hi, pair_lo[:, count:])
-        + dot_nn(turned_lo, pair_hi[:, count:])
-    )
+    with_high = dot_nn(turned, pair_hi[:, count:])
+    cross = with_high[:count] + with_high[count:] + dot_nn(rowx_hi[...], pair_lo[:, count:])
     sq_dist = row_sq[:, 0:1] + jnp.concatenate(col_sq, axis=1) - 2.0 * gram
     radius = jnp.sqrt(jnp.maximum(sq_dist, 0.0))
     envelope = outer_factor * jnp.exp(-decay_rate * radius)
@@ -207,7 +200,9 @@
     def multiply(first, end):
         at = slice((first - 1) * GROUP, ROWS if end == 9 else (end - 1) * GROUP)
         part_hi, part_lo = pair_hi[at, :], pair_lo[at, :]
-        grads[at, :] = dot_nt(part_hi, high) + dot_nt(part_lo, high) + dot_nt(part_hi, low)
+        both = dot_nt(jnp.concatenate([part_hi, part_lo], axis=0), high)
+        size = part_hi.shape[0]
+        grads[at, :] = both[:size] + both[size:] + dot_nt(part_hi, low)
 
     def terms_of(t, d):
         at, lanes = rows_of(d), slice(t * LANES, (t + 1) * LANES)

time: 46.1 us -> 45.6 us (0.989)
  no operation moved by 1% of the time
where the time goes in v7:
time: 45.6 us; the launch traced here: 45.3 us
  blocking collectives  18.5 us (41%)
  starting transfers between devices  15 us (33%)
  Pallas kernels  5.9 us (13%)
  waiting for transfers between devices  3.37 us (7%)
  local copies, waits for them, and re-layouts  1.59 us (3%)
  other arithmetic  0.86 us (2%)
    all_to_all x1, starting transfers between devices, exchange(): return lax.all_to_all(value, axis, split_axis=0, concat_axis=0, tiled=True)  11.6 us
    all_to_all x1, blocking collectives, exchange(): return lax.all_to_all(value, axis, split_axis=0, concat_axis=0, tiled=True)  10.6 us
    all_gather x1, blocking collectives, in_groups(): lax.all_gather(value, axis, axis=0, tiled=True, axis_index_groups=groups)  7.94 us
    pallas_call x1, Pallas kernels, cols_apply(): pl.pallas_call(functools.partial(apply_kernel, place), out_shape=shape(LA...  4.51 us
    ppermute x3, starting transfers between devices, with_partners(): lax.ppermute(value, axis, [(n, n ^ step) for n in range(count)])  3.44 us
    ppermute x3, waiting for transfers between devices, with_partners(): lax.ppermute(value, axis, [(n, n ^ step) for n in range(count)])  3.37 us
    pallas_call x1, Pallas kernels, row_terms(): pl.pallas_call(rows_kernel, out_shape=(shape(ROWS, LANES), shape(2, 3, WR...  1.39 us
  transfers between devices with their start and end apart: 4, of which 2 were waited for; matrix products, arithmetic and copies ran while one was open for 0% of the time, Pallas kernels for 3%

profile of v7, /device:TPU:1, one launch (start us, length us, event | category | flops | bytes accessed | tf_op | source)
XLA Modules:
  0.0 45.3 jit_solution(9770118409799518863)
XLA Ops:
  0.0 0.7 %fusion = (f32[8,147]{1,0:T(8,128)S(1)}, f32[8,147]{1,0:T(8,128)S(1)}, f32[8,147]{1,0:T(8,128)S(1)}, f32[8,147]{1,0:T(8,128)S(1)}) fusion(f32[16,147]{1,0:T(8,128)} %param.4, f32[16,147]{1,0:T(8,128)} %param.5), kind=kLoop, calls=%fused_computation.4 | loop fusion | bytes 37632 | tf_op jit(solution)/shard_map/slice | solution.py:325
  0.8 0.1 pad_maximum_fusion.1
  0.8 0.8 %broadcast_in_dim.3 = f32[16,8,588]{2,1,0:T(8,128)} broadcast(f32[8,588]{1,0:T(8,128)S(1)} %pad_maximum_fusion.1), dimensions={1,2} | broadcast | bytes 319872 | tf_op jit(solution)/shard_map/broadcast_in_dim | solution.py:333
  1.6 11.6 %all-to-all-start = ((f32[16,8,588]{2,1,0:T(8,128)}), f32[16,8,588]{2,1,0:T(8,128)S(1)}, u32[]{:S(2)}, u32[]{:S(2)}) async-start(f32[16,8,588]{2,1,0:T(8,128)} %broadcast_in_dim.3), calls=%async_computation | async-start | bytes 655360 | tf_op jit(solution)/shard_map/all_to_all | solution.py:329
  13.2 0.0 copy-start.1
  13.2 0.1 pad_maximum_fusion.3
  13.3 2.8 %collective-permute-start.2 = (f32[8,294]{1,0:T(8,128)S(1)}, f32[8,294]{1,0:T(8,128)S(1)}, u32[]{:S(2)}, u32[]{:S(2)}) collective-permute-start(f32[8,294]{1,0:T(8,128)S(1)} %pad_maximum_fusion.3), channel_id=1, source_target_pairs={{0,192},{16,208},{32,224},{48,240},{64,128},{80,144},{96,160},{112... | collective-permute-start | bytes 28232 | tf_op jit(solution)/shard_map/ppermute | solution.py:344
  16.0 0.3 collective-permute-start.1
  16.4 0.3 collective-permute-start
  16.7 0.0 copy-done.1
  16.7 0.4 collective-permute-done.2
  17.1 3.0 %collective-permute-done.1 = f32[8,294]{1,0:T(8,128)S(1)} collective-permute-done((f32[8,294]{1,0:T(8,128)S(1)}, f32[8,294]{1,0:T(8,128)S(1)}, u32[]{:S(2)}, u32[]{:S(2)}) %collective-permute-start.1) | collective-permute-done | bytes 9440 | tf_op jit(solution)/shard_map/ppermute | solution.py:344
  20.1 0.0 collective-permute-done
  20.1 0.1 pad_maximum_fusion
  20.1 0.0 copy-start
  20.1 7.9 %all_gather.3.rows_ref = f32[128,294]{1,0:T(8,128)S(1)} all-gather(f32[32,294]{1,0:T(8,128)S(1)} %pad_maximum_fusion), channel_id=1, replica_groups={{0,16,32,48},{64,80,96,112},{128,144,160,176},{192,208,224,240},{1,17,3..., dimensions={0}, use_global_device_ids=true | all-gather | bytes 188160 | tf_op jit(solution)/shard_map/all_gather | solution.py:339
  28.1 0.0 copy-done
  28.1 1.4 %shard_map.46 = (f32[1184,128]{1,0:T(8,128)S(1)}, f32[2,3,72,128]{3,2,1,0:T(8,128)S(1)}, bf16[256,1184]{1,0:T(8,128)(2,1)S(1)}, bf16[256,1184]{1,0:T(8,128)(2,1)S(1)}, f32[256,128]{1,0:T(8,128)S(1)}) custom-call(f32[128,294]{1,0:T(8,128)S(1)} %all_gather.3.rows_ref, s32[2,1176]{1,0:T(2,128)S(1)} %copy-done, f32[1,1176]{1,0:T(1,128)S(1)} %reshape.10.pair_scale_ref), custom_call_target="tpu_custom_call" | custom-call | flops 40000000 | bytes 6000000 | tf_op jit(solution)/shard_map/pallas_call | solution.py:271
  29.5 0.0 all-to-all-done
  29.5 4.5 %shard_map.47 = f32[128,294]{1,0:T(8,128)S(1)} custom-call(f32[128,588]{1,0:T(8,128)S(1)} %bitcast.2, f32[1184,128]{1,0:T(8,128)S(1)} %get-tuple-element.10.scale_ref, f32[2,3,72,128]{3,2,1,0:T(8,128)S(1)} %get-tuple-element.11.rows_w, bf16[256,1184]{1,0:T(8,128)(2,1)S(1)} %get-tuple-element.12.rowx_hi, bf16[256,1184]{1,0:T(8,128)(2,1)S(1)} %get-tuple-element.13.rowx_lo, ...), custom_call_target="tpu_custom_call" | custom-call | flops 2000000000 | bytes 6000000 | tf_op jit(solution)/shard_map/pallas_call | solution.py:291
  34.0 10.6 %all_to_all.10 = f32[16,8,294]{2,1,0:T(8,128)S(1)} all-to-all(f32[16,8,294]{2,1,0:T(8,128)S(1)} %bitcast.3), channel_id=1, replica_groups=mesh['row'=16,'col'=16] {'row'}, dimensions={0} | all-to-all | bytes 301056 | tf_op jit(solution)/shard_map/all_to_all | solution.py:329
  44.6 0.1 fusion.2
  44.7 0.6 %pad_maximum_fusion.2 = f32[16,147]{1,0:T(8,128)} fusion(f32[8,147]{1,0:T(8,128)S(1)} %get-tuple-element.20, f32[8,147]{1,0:T(8,128)S(1)} %get-tuple-element.19), kind=kLoop, calls=%fused_computation.2 | loop fusion | flops 2352 | bytes 18816 | tf_op jit(solution)/shard_map/concatenate | solution.py:366
  (2 shorter events, 0.0 us)
Async XLA Ops:
  1.6 27.9 %all-to-all-start = ((f32[16,8,588]{2,1,0:T(8,128)}), f32[16,8,588]{2,1,0:T(8,128)S(1)}, u32[]{:S(2)}, u32[]{:S(2)}) async-start(f32[16,8,588]{2,1,0:T(8,128)} %broadcast_in_dim.3), calls=%async_computation | async-start | bytes 655360 | tf_op jit(solution)/shard_map/all_to_all | solution.py:329
  13.2 3.5 %copy-start.1 = (f32[1176]{0:T(1024)S(1)}, f32[1176]{0:T(1024)}, u32[]{:S(2)}) copy-start(f32[1176]{0:T(1024)} %param.7) | copy-start | bytes 14116
  13.3 3.8 %collective-permute-start.2 = (f32[8,294]{1,0:T(8,128)S(1)}, f32[8,294]{1,0:T(8,128)S(1)}, u32[]{:S(2)}, u32[]{:S(2)}) collective-permute-start(f32[8,294]{1,0:T(8,128)S(1)} %pad_maximum_fusion.3), channel_id=1, source_target_pairs={{0,192},{16,208},{32,224},{48,240},{64,128},{80,144},{96,160},{112... | collective-permute-start | bytes 28232 | tf_op jit(solution)/shard_map/ppermute | solution.py:344
  16.0 4.0 %collective-permute-start.1 = (f32[8,294]{1,0:T(8,128)S(1)}, f32[8,294]{1,0:T(8,128)S(1)}, u32[]{:S(2)}, u32[]{:S(2)}) collective-permute-start(f32[8,294]{1,0:T(8,128)S(1)} %pad_maximum_fusion.3), channel_id=1, source_target_pairs={{0,128},{16,144},{32,160},{48,176},{64,192},{80,208},{96,224},{112... | collective-permute-start | bytes 28232 | tf_op jit(solution)/shard_map/ppermute | solution.py:344
  16.4 3.7 %collective-permute-start = (f32[8,294]{1,0:T(8,128)S(1)}, f32[8,294]{1,0:T(8,128)S(1)}, u32[]{:S(2)}, u32[]{:S(2)}) collective-permute-start(f32[8,294]{1,0:T(8,128)S(1)} %pad_maximum_fusion.3), channel_id=1, source_target_pairs={{0,64},{16,80},{32,96},{48,112},{64,0},{80,16},{96,32},{112,48},{1... | collective-permute-start | bytes 28232 | tf_op jit(solution)/shard_map/ppermute | solution.py:344
  20.1 7.9 %copy-start = (s32[2,1176]{1,0:T(2,128)S(1)}, s32[2,1176]{1,0:T(2,128)}, u32[]{:S(2)}) copy-start(s32[2,1176]{1,0:T(2,128)} %pairs_ref.1) | copy-start | bytes 28228

commit v8 on v7

--- a/solution.py
+++ b/solution.py
@@ -106,11 +106,10 @@
 
 
 def rows_kernel(
-    rows_ref, pairs_ref, pair_scale_ref,
-    scale_ref, rows_w, rowx_hi, rowx_lo, row_sq,
+    rows_ref, scale_ref,
+    rows_w, rowx_hi, rowx_lo, row_sq,
     flat_rows, row_x,
 ):
-    spread_scale(pairs_ref, pair_scale_ref, scale_ref)
     flat_rows[...] = rows_ref[...].T
     for t in range(2):
         wrap_rows(flat_rows, t * CART, rows_w, t)
@@ -267,24 +266,38 @@
 params = pltpu.CompilerParams(vmem_limit_bytes=16 * 1024 * 1024)
 
 
+def scale_table(atom_pairs, pair_scale):
+    return pl.pallas_call(
+        spread_scale,
+        out_shape=shape(ROWS, LANES),
+        in_specs=vmem(2),
+        out_specs=vmem(1)[0],
+        compiler_params=params,
+        cost_estimate=pl.CostEstimate(
+            flops=20_000_000, bytes_accessed=700_000, transcendentals=0
+        ),
+    )(atom_pairs, pair_scale.reshape(1, -1))
+
+
 def row_terms(rows, atom_pairs, pair_scale):
-    return pl.pallas_call(
+    scale = scale_table(atom_pairs, pair_scale)
+    terms = pl.pallas_call(
         rows_kernel,
         out_shape=(
-            shape(ROWS, LANES),
             shape(2, 3, WRAP, LANES),
             shape(2 * LANES, KDIM, kind=bf16),
             shape(2 * LANES, KDIM, kind=bf16),
             shape(2 * LANES, LANES),
         ),
-        in_specs=vmem(3),
-        out_specs=tuple(vmem(5)),
+        in_specs=vmem(2),
+        out_specs=tuple(vmem(4)),
         scratch_shapes=[pltpu.VMEM((2 * CART, LANES), f32), pltpu.VMEM((2, ROWS, LANES), f32)],
         compiler_params=params,
         cost_estimate=pl.CostEstimate(
             flops=40_000_000, bytes_accessed=6_000_000, transcendentals=300_000
         ),
-    )(rows, atom_pairs, pair_scale.reshape(1, -1))
+    )(rows, scale)
+    return scale, *terms
 
 
 def cols_apply(cols, terms, place):

time: 45.6 us -> 45.6 us (level)
  waiting for transfers between devices: 3.37 us -> 2.79 us
    ppermute x3, waiting for transfers between devices: 3.37 us -> 2.79 us  [with_partners(): lax.ppermute(value, axis, [(n, n ^ step) for n in range(count)])]
    all_to_all x1, blocking collectives: 10.6 us -> 11.1 us  [exchange(): return lax.all_to_all(value, axis, split_axis=0, concat_axis=0, tiled=True)]
    pallas_call x1 -> x2, Pallas kernels: 1.39 us -> 1.64 us  [the longest x1 1.07 us: row_terms(): pl.pallas_call(rows_kernel, out_shape=(shape(2, 3, WRAP, LANES), shape(2...]
  transfers between devices with their start and end apart: 4 -> 4, of which waited for: 2 -> 1; matrix products, arithmetic and copies ran while one was open for 0% -> 0% of each run, Pallas kernels for 3% -> 4%
where the time goes in v8:
time: 45.6 us; the launch traced here: 45.4 us
  blocking collectives  18.9 us (41%)
  starting transfers between devices  15 us (33%)
  Pallas kernels  6.15 us (13%)
  waiting for transfers between devices  2.79 us (6%)
  local copies, waits for them, and re-layouts  1.59 us (3%)
  other arithmetic  0.86 us (2%)
    all_to_all x1, starting transfers between devices, exchange(): return lax.all_to_all(value, axis, split_axis=0, concat_axis=0, tiled=True)  11.6 us
    all_to_all x1, blocking collectives, exchange(): return lax.all_to_all(value, axis, split_axis=0, concat_axis=0, tiled=True)  11.1 us
    all_gather x1, blocking collectives, in_groups(): lax.all_gather(value, axis, axis=0, tiled=True, axis_index_groups=groups)  7.81 us
    pallas_call x1, Pallas kernels, cols_apply(): pl.pallas_call(functools.partial(apply_kernel, place), out_shape=shape(LA...  4.51 us
    ppermute x3, starting transfers between devices, with_partners(): lax.ppermute(value, axis, [(n, n ^ step) for n in range(count)])  3.45 us
    ppermute x3, waiting for transfers between devices, with_partners(): lax.ppermute(value, axis, [(n, n ^ step) for n in range(count)])  2.79 us
    pallas_call x1, Pallas kernels, row_terms(): pl.pallas_call(rows_kernel, out_shape=(shape(2, 3, WRAP, LANES), shape(2...  1.07 us
  transfers between devices with their start and end apart: 4, of which 1 were waited for; matrix products, arithmetic and copies ran while one was open for 0% of the time, Pallas kernels for 4%

profile of v8, /device:TPU:1, one launch (start us, length us, event | category | flops | bytes accessed | tf_op | source)
XLA Modules:
  0.0 45.4 jit_solution(16456446290767572588)
XLA Ops:
  0.0 0.7 %fusion = (f32[8,147]{1,0:T(8,128)S(1)}, f32[8,147]{1,0:T(8,128)S(1)}, f32[8,147]{1,0:T(8,128)S(1)}, f32[8,147]{1,0:T(8,128)S(1)}) fusion(f32[16,147]{1,0:T(8,128)} %param.4, f32[16,147]{1,0:T(8,128)} %param.5), kind=kLoop, calls=%fused_computation.4 | loop fusion | bytes 37632 | tf_op jit(solution)/shard_map/slice | solution.py:338
  0.8 0.1 pad_maximum_fusion.1
  0.8 0.8 %broadcast_in_dim.3 = f32[16,8,588]{2,1,0:T(8,128)} broadcast(f32[8,588]{1,0:T(8,128)S(1)} %pad_maximum_fusion.1), dimensions={1,2} | broadcast | bytes 319872 | tf_op jit(solution)/shard_map/broadcast_in_dim | solution.py:346
  1.6 11.6 %all-to-all-start = ((f32[16,8,588]{2,1,0:T(8,128)}), f32[16,8,588]{2,1,0:T(8,128)S(1)}, u32[]{:S(2)}, u32[]{:S(2)}) async-start(f32[16,8,588]{2,1,0:T(8,128)} %broadcast_in_dim.3), calls=%async_computation | async-start | bytes 655360 | tf_op jit(solution)/shard_map/all_to_all | solution.py:342
  13.2 0.0 copy-start.1
  13.2 0.1 pad_maximum_fusion.3
  13.3 0.0 copy-start
  13.3 2.8 %collective-permute-start.2 = (f32[8,294]{1,0:T(8,128)S(1)}, f32[8,294]{1,0:T(8,128)S(1)}, u32[]{:S(2)}, u32[]{:S(2)}) collective-permute-start(f32[8,294]{1,0:T(8,128)S(1)} %pad_maximum_fusion.3), channel_id=1, source_target_pairs={{0,192},{16,208},{32,224},{48,240},{64,128},{80,144},{96,160},{112... | collective-permute-start | bytes 28232 | tf_op jit(solution)/shard_map/ppermute | solution.py:357
  16.0 0.3 collective-permute-start.1
  16.4 0.3 collective-permute-start
  16.7 0.0 copy-done.1
  16.7 0.0 copy-done
  16.7 0.6 %shard_map.46.scale_ref = f32[1184,128]{1,0:T(8,128)S(1)} custom-call(s32[2,1176]{1,0:T(2,128)S(1)} %copy-done, f32[1,1176]{1,0:T(1,128)S(1)} %reshape.10.scale_ref), custom_call_target="tpu_custom_call" | custom-call | flops 20000000 | bytes 700000 | tf_op jit(solution)/shard_map/pallas_call | solution.py:270
  17.3 0.0 collective-permute-done.2
  17.3 2.8 %collective-permute-done.1 = f32[8,294]{1,0:T(8,128)S(1)} collective-permute-done((f32[8,294]{1,0:T(8,128)S(1)}, f32[8,294]{1,0:T(8,128)S(1)}, u32[]{:S(2)}, u32[]{:S(2)}) %collective-permute-start.1) | collective-permute-done | bytes 9440 | tf_op jit(solution)/shard_map/ppermute | solution.py:357
  20.1 0.0 collective-permute-done
  20.1 0.1 pad_maximum_fusion
  20.2 7.8 %all_gather.3.rows_ref = f32[128,294]{1,0:T(8,128)S(1)} all-gather(f32[32,294]{1,0:T(8,128)S(1)} %pad_maximum_fusion), channel_id=1, replica_groups={{0,16,32,48},{64,80,96,112},{128,144,160,176},{192,208,224,240},{1,17,3..., dimensions={0}, use_global_device_ids=true | all-gather | bytes 188160 | tf_op jit(solution)/shard_map/all_gather | solution.py:352
  28.0 1.1 %shard_map.47 = (f32[2,3,72,128]{3,2,1,0:T(8,128)S(1)}, bf16[256,1184]{1,0:T(8,128)(2,1)S(1)}, bf16[256,1184]{1,0:T(8,128)(2,1)S(1)}, f32[256,128]{1,0:T(8,128)S(1)}) custom-call(f32[128,294]{1,0:T(8,128)S(1)} %all_gather.3.rows_ref, f32[1184,128]{1,0:T(8,128)S(1)} %shard_map.46.scale_ref), custom_call_target="tpu_custom_call" | custom-call | flops 40000000 | bytes 6000000 | tf_op jit(solution)/shard_map/pallas_call | solution.py:284
  29.1 0.0 all-to-all-done
  29.1 4.5 %shard_map.48 = f32[128,294]{1,0:T(8,128)S(1)} custom-call(f32[128,588]{1,0:T(8,128)S(1)} %bitcast.2, f32[1184,128]{1,0:T(8,128)S(1)} %shard_map.46.scale_ref, f32[2,3,72,128]{3,2,1,0:T(8,128)S(1)} %get-tuple-element.9.rows_w, bf16[256,1184]{1,0:T(8,128)(2,1)S(1)} %get-tuple-element.10.rowx_hi, bf16[256,1184]{1,0:T(8,128)(2,1)S(1)} %get-tuple-element.11.rowx_lo, ...), custom_call_target="tpu_custom_call" | custom-call | flops 2000000000 | bytes 6000000 | tf_op jit(solution)/shard_map/pallas_call | solution.py:304
  33.6 11.1 %all_to_all.10 = f32[16,8,294]{2,1,0:T(8,128)S(1)} all-to-all(f32[16,8,294]{2,1,0:T(8,128)S(1)} %bitcast.3), channel_id=1, replica_groups=mesh['row'=16,'col'=16] {'row'}, dimensions={0} | all-to-all | bytes 301056 | tf_op jit(solution)/shard_map/all_to_all | solution.py:342
  44.7 0.1 fusion.2
  44.7 0.6 %pad_maximum_fusion.2 = f32[16,147]{1,0:T(8,128)} fusion(f32[8,147]{1,0:T(8,128)S(1)} %get-tuple-element.18, f32[8,147]{1,0:T(8,128)S(1)} %get-tuple-element.17), kind=kLoop, calls=%fused_computation.2 | loop fusion | flops 2352 | bytes 18816 | tf_op jit(solution)/shard_map/concatenate | solution.py:379
  (2 shorter events, 0.0 us)
Async XLA Ops:
  1.6 27.5 %all-to-all-start = ((f32[16,8,588]{2,1,0:T(8,128)}), f32[16,8,588]{2,1,0:T(8,128)S(1)}, u32[]{:S(2)}, u32[]{:S(2)}) async-start(f32[16,8,588]{2,1,0:T(8,128)} %broadcast_in_dim.3), calls=%async_computation | async-start | bytes 655360 | tf_op jit(solution)/shard_map/all_to_all | solution.py:342
  13.2 3.5 %copy-start.1 = (f32[1176]{0:T(1024)S(1)}, f32[1176]{0:T(1024)}, u32[]{:S(2)}) copy-start(f32[1176]{0:T(1024)} %param.7) | copy-start | bytes 14116
  13.3 3.5 %copy-start = (s32[2,1176]{1,0:T(2,128)S(1)}, s32[2,1176]{1,0:T(2,128)}, u32[]{:S(2)}) copy-start(s32[2,1176]{1,0:T(2,128)} %pairs_ref.1) | copy-start | bytes 28228
  13.3 4.0 %collective-permute-start.2 = (f32[8,294]{1,0:T(8,128)S(1)}, f32[8,294]{1,0:T(8,128)S(1)}, u32[]{:S(2)}, u32[]{:S(2)}) collective-permute-start(f32[8,294]{1,0:T(8,128)S(1)} %pad_maximum_fusion.3), channel_id=1, source_target_pairs={{0,192},{16,208},{32,224},{48,240},{64,128},{80,144},{96,160},{112... | collective-permute-start | bytes 28232 | tf_op jit(solution)/shard_map/ppermute | solution.py:357
  16.0 4.0 %collective-permute-start.1 = (f32[8,294]{1,0:T(8,128)S(1)}, f32[8,294]{1,0:T(8,128)S(1)}, u32[]{:S(2)}, u32[]{:S(2)}) collective-permute-start(f32[8,294]{1,0:T(8,128)S(1)} %pad_maximum_fusion.3), channel_id=1, source_target_pairs={{0,128},{16,144},{32,160},{48,176},{64,192},{80,208},{96,224},{112... | collective-permute-start | bytes 28232 | tf_op jit(solution)/shard_map/ppermute | solution.py:357
  16.4 3.7 %collective-permute-start = (f32[8,294]{1,0:T(8,128)S(1)}, f32[8,294]{1,0:T(8,128)S(1)}, u32[]{:S(2)}, u32[]{:S(2)}) collective-permute-start(f32[8,294]{1,0:T(8,128)S(1)} %pad_maximum_fusion.3), channel_id=1, source_target_pairs={{0,64},{16,80},{32,96},{48,112},{64,0},{80,16},{96,32},{112,48},{1... | collective-permute-start | bytes 28232 | tf_op jit(solution)/shard_map/ppermute | solution.py:357
